TPU v7x, 32 devices: a whole 2x2x4 slice. The times are simulated.
32 devices in a mesh: az: 4 (over x, core), rg: 8 (over z, y).
Axes of the slice: x: 2, y: 2, z: 4, core: 2. Of those that a mesh axis runs over, the one named last changes fastest.
Arguments:
- reference_image: bfloat16 [2, 512, 2048], P(None, 'az', 'rg'), may hold values from -600 to 600, as said below
- secondary_image: bfloat16 [2, 512, 2048], P(None, 'az', 'rg'), may hold values from -600 to 600, as said below
- block_shifts: int32 [2, 8, 32], P(None, 'az', 'rg'), may hold values from -8 to 8
- shift_bins: int32 [2, 8, 32], P(None, 'az', 'rg'), may hold values from 0 to 15
- land_mask: int32 [8, 32], P('az', 'rg'), may hold values from 0 to 1, as said below
- coarse_peaks: int32 [2, 8, 32], P(None, 'az', 'rg'), may hold values from -29 to 27
Outputs:
- correlation_surface: float32 [8, 32, 4096], P('az', 'rg')
- peak_patch: float32 [8, 32, 1024], P('az', 'rg')
Inputs may be any that keep to these rules, and one draw needn't show every extreme that they name: `reference_image`: real and imaginary parts of a radar scene, magnitudes at most 600. `secondary_image`: the same scene seen a second time, magnitudes at most 600. `land_mask`: the share of land chips varies from tile to tile (a tile is the 2 x 4 chips of one device), and at least one tile is all land.
All inputs are finite; a program needn't handle non-finite values.
Results may differ from a plain program's by a relative error of at most 0.013.
Values may be sent and summed in bfloat16 or wider, within the bound.
A program may use at most 64 MiB of HBM per device.

v0:
```python
import jax
import jax.numpy as jnp
from jax import lax
from jax.sharding import PartitionSpec as P

CHIP = 64
SEARCH = 32
TAPS = 8
NBIN = 16
OVERS = 16
PATCH = 8
REACH = 12


epsilon = 1e-06


def padded_2(cells, sides, width):
    for axis, dim in sides:
        count = lax.axis_size(axis)
        ends = count - 1
        head = lax.slice_in_dim(cells, 0, width, axis=dim)
        tail = lax.slice_in_dim(cells, cells.shape[dim] - width, cells.shape[dim], axis=dim)
        cells = jnp.concatenate(
            [
                lax.ppermute(tail, axis, [(i, (i + 1) % count) for i in range(ends)]),
                cells,
                lax.ppermute(head, axis, [((i + 1) % count, i) for i in range(ends)]),
            ],
            axis=dim,
        )
    return cells


def lanczos(offset):
    half_taps = TAPS // 2
    inside = jnp.abs(offset) < half_taps
    return jnp.where(inside, jnp.sinc(offset) * jnp.sinc(offset / half_taps), 0.0)


def kernel_table():
    fraction = jnp.arange(NBIN).astype(jnp.float32) / NBIN
    tap_index = jnp.arange(TAPS).astype(jnp.float32)
    offset = tap_index[None, :] - (TAPS // 2 - 1) - fraction[:, None]
    return lanczos(offset).astype(jnp.bfloat16)


def patch_table():
    sample_at = (jnp.arange(2 * OVERS).astype(jnp.float32) - OVERS) / OVERS
    node_at = jnp.arange(PATCH).astype(jnp.float32) - (PATCH // 2 - 1)
    return lanczos(sample_at[:, None] - node_at[None, :]).astype(jnp.float32)


def kernel_rows(kernel, bin_index):
    matches = bin_index[:, None, None] == jnp.arange(NBIN)[None, :, None]
    return jnp.sum(jnp.where(matches, kernel.astype(jnp.float32)[None], 0.0), axis=1)


def shifted_band(taps_rows, shift_values):
    span = CHIP + 2 * REACH
    offset = jnp.arange(span)[None, :] - jnp.arange(CHIP)[:, None] - 1 - REACH + TAPS // 2
    offset = offset[None] - shift_values[:, None, None]
    running = jnp.zeros((taps_rows.shape[0], CHIP, span), jnp.float32)
    for tap_index in range(TAPS):
        running = running + jnp.where(
            offset == tap_index, taps_rows[:, tap_index][:, None, None], 0.0
        )
    return running.astype(jnp.bfloat16)


def resample_grid(source, kernel, shifts, bins, block_lines, block_columns):
    lead = CHIP - REACH
    padded = jnp.pad(source, ((0, 0), (lead, lead), (lead, lead)))
    line_pieces = padded.reshape(2, block_lines + 2, CHIP, padded.shape[2])
    line_blocks = jnp.concatenate(
        [line_pieces[:, :-2, CHIP - REACH :], line_pieces[:, 1:-1], line_pieces[:, 2:, :REACH]],
        axis=2,
    )
    column_pieces = line_blocks.reshape(2, block_lines, CHIP + 2 * REACH, block_columns + 2, CHIP)
    blocks = jnp.concatenate(
        [
            column_pieces[..., :-2, CHIP - REACH :],
            column_pieces[..., 1:-1, :],
            column_pieces[..., 2:, :REACH],
        ],
        axis=4,
    )
    band_rows = shifted_band(
        kernel_rows(kernel, bins[0].reshape(-1)), shifts[0].reshape(-1)
    ).reshape(block_lines, block_columns, CHIP, CHIP + 2 * REACH)
    band_columns = shifted_band(
        kernel_rows(kernel, bins[1].reshape(-1)), shifts[1].reshape(-1)
    ).reshape(block_lines, block_columns, CHIP, CHIP + 2 * REACH)
    half_done = jnp.einsum(
        "uvij,cujvk->cuvik", band_rows, blocks, preferred_element_type=jnp.float32
    ).astype(jnp.bfloat16)
    second = jnp.einsum(
        "cuvik,uvlk->cuivl", half_done, band_columns, preferred_element_type=jnp.float32
    )
    block_amplitude = jnp.sqrt(second[0] * second[0] + second[1] * second[1]).astype(jnp.bfloat16)
    return block_amplitude.reshape(block_lines * CHIP, block_columns * CHIP)


def surfaces(chip_data, window_data):
    group_size = chip_data.shape[0]
    chip_float = chip_data.reshape(group_size, CHIP, CHIP).astype(jnp.float32)
    centred = (chip_float - jnp.mean(chip_float, axis=(1, 2), keepdims=True)).astype(jnp.bfloat16)
    centred_float = centred.astype(jnp.float32)
    energy = jnp.sum(centred_float * centred_float, axis=(1, 2))
    window = window_data.reshape(group_size, 2 * CHIP, 2 * CHIP)
    lag_index = jnp.arange(CHIP)
    column_index = jnp.arange(2 * CHIP)
    hankel = window[:, lag_index[:, None] + lag_index[None, :], :]
    column_gap = column_index[None, :] - lag_index[:, None]
    spread = jnp.pad(centred, ((0, 0), (0, 0), (0, CHIP)))
    toeplitz = spread[:, :, jnp.where((column_gap >= 0) & (column_gap < CHIP), column_gap, CHIP)]
    product_sum = jnp.einsum("gaiq,gidq->gad", hankel, toeplitz, preferred_element_type=jnp.float32)
    ones_band = (
        (column_index[None, :] >= lag_index[:, None])
        & (column_index[None, :] < lag_index[:, None] + CHIP)
    ).astype(jnp.float32)
    window_float = window.astype(jnp.float32)
    both_terms = jnp.stack([window_float, window_float * window_float], axis=1)
    row_sums = jnp.einsum("ap,gspq->gsaq", ones_band, both_terms, precision=lax.Precision.HIGHEST)
    box_sums = jnp.einsum("gsaq,dq->gsad", row_sums, ones_band, precision=lax.Precision.HIGHEST)
    window_sum = box_sums[:, 0]
    squares = box_sums[:, 1]
    chip_area = CHIP * CHIP
    normed = product_sum / jnp.sqrt(
        energy[:, None, None] * (squares - window_sum * window_sum / chip_area) + epsilon
    )
    return normed.reshape(group_size, chip_area)


def compact_list(land_flags):
    slot_total = land_flags.shape[0]
    chip_rank = jnp.cumsum(land_flags) - 1
    land_count = jnp.sum(land_flags)
    slot_index = jnp.arange(slot_total)
    matches = (land_flags[None, :] == 1) & (chip_rank[None, :] == slot_index[:, None])
    chip_order = jnp.sum(jnp.where(matches, slot_index[None, :], 0), axis=1)
    return (chip_order, land_count, chip_rank)


def run_chips(chip_data, window_data, chip_order, land_count):
    slot_total = chip_data.shape[0]
    group_size = min(4, slot_total)
    results = jnp.zeros((slot_total, CHIP * CHIP), jnp.float32)
    turn_count = (land_count + group_size - 1) // group_size

    def one_turn(turn_index, running):
        positions = turn_index * group_size + jnp.arange(group_size)
        picked = jnp.take(chip_order, jnp.minimum(positions, slot_total - 1), mode="clip")
        block_values = surfaces(
            jnp.take(chip_data, picked, axis=0, mode="clip"),
            jnp.take(window_data, picked, axis=0, mode="clip"),
        )
        target_rows = jnp.where(positions < land_count, picked, slot_total)
        return running.at[target_rows].set(block_values, mode="drop")

    return lax.fori_loop(0, turn_count, one_turn, results)


def oversample(surface, peak_pair, lobes):
    lead_offset = PATCH // 2 - 1
    start_rows = peak_pair[0] + SEARCH - lead_offset
    start_columns = peak_pair[1] + SEARCH - lead_offset

    def cut_patch(field_plane, row_start, column_start):
        return lax.dynamic_slice(field_plane, (row_start, column_start), (PATCH, PATCH))

    nearby = jax.vmap(cut_patch)(surface, start_rows, start_columns)
    patch_values = jnp.einsum(
        "tk,gkl,ul->gtu", lobes, nearby, lobes, precision=lax.Precision.HIGHEST
    )
    return patch_values.reshape(surface.shape[0], 4 * OVERS * OVERS)


def per_device(reference_image, secondary_image, block_shifts, shift_bins, land_mask, coarse_peaks):
    along_lines, along_columns = land_mask.shape
    slot_count = along_lines * along_columns
    chip_area = CHIP * CHIP
    kernel = kernel_table()
    extended = padded_2(secondary_image, (("az", 1), ("rg", 2)), REACH)
    amplitude = resample_grid(
        extended, kernel, block_shifts, shift_bins, along_lines, along_columns
    )
    padded_amplitude = padded_2(amplitude, (("az", 0), ("rg", 1)), SEARCH)
    pieces = padded_amplitude.reshape(along_lines + 1, CHIP, along_columns + 1, CHIP).transpose(
        0, 2, 1, 3
    )
    upper_half = jnp.concatenate([pieces[:-1, :-1], pieces[:-1, 1:]], axis=3)
    lower_half = jnp.concatenate([pieces[1:, :-1], pieces[1:, 1:]], axis=3)
    windows = jnp.concatenate([upper_half, lower_half], axis=2).reshape(slot_count, 4 * chip_area)
    reference_float = reference_image.astype(jnp.float32)
    reference_amplitude = jnp.sqrt(
        reference_float[0] * reference_float[0] + reference_float[1] * reference_float[1]
    ).astype(jnp.bfloat16)
    chip_data = (
        reference_amplitude.reshape(along_lines, CHIP, along_columns, CHIP)
        .transpose(0, 2, 1, 3)
        .reshape(slot_count, chip_area)
    )
    land_flags = land_mask.reshape(-1)
    chip_order, land_count, chip_rank = compact_list(land_flags)
    surface = run_chips(chip_data, windows, chip_order, land_count)
    lobes = patch_table()
    peak_pair = coarse_peaks.reshape(2, slot_count)
    patch_values = oversample(surface.reshape(slot_count, CHIP, CHIP), peak_pair, lobes)
    return (
        surface.reshape(along_lines, along_columns, chip_area),
        patch_values.reshape(along_lines, along_columns, 4 * OVERS * OVERS),
    )


def solution(mesh):
    in_specs = (
        P(None, "az", "rg"),
        P(None, "az", "rg"),
        P(None, "az", "rg"),
        P(None, "az", "rg"),
        P("az", "rg"),
        P(None, "az", "rg"),
    )
    out_specs = (P("az", "rg", None), P("az", "rg", None))
    return jax.shard_map(
        per_device, mesh=mesh, in_specs=in_specs, out_specs=out_specs, check_vma=False
    )
```

profile of v0, /device:TPU:25, one launch (start us, length us, event | category | flops | bytes accessed | tf_op | source)
XLA Modules:
  0.0 282.3 jit_solution(5726037422394896156)
XLA Ops:
  1.4 2.6 collective-permute-start.1
  4.0 3.0 %collective-permute-start = (bf16[2,12,256]{2,1,0:T(8,128)(2,1)S(1)}, bf16[2,12,256]{2,1,0:T(8,128)(2,1)S(1)}, u32[]{:S(2)}, u32[]{:S(2)}) collective-permute-start(bf16[2,12,256]{2,1,0:T(8,128)(2,1)S(1)} %get-tuple-element.158), channel_id=1, source_target_pairs={{0,8},{8,16},{16,24},{1,9},{9,17},{17,25},{2,10},{10,18},{18,26},{... | collective-permute-start | bytes 36872 | tf_op jit(solution)/shard_map/ppermute | solution.py:26
  14.1 3.0 %collective-permute-start.3 = (bf16[2,152,12]{2,1,0:T(8,128)(2,1)S(1)}, bf16[2,152,12]{2,1,0:T(8,128)(2,1)S(1)}, u32[]{:S(2)}, u32[]{:S(2)}) collective-permute-start(bf16[2,152,12]{2,1,0:T(8,128)(2,1)S(1)} %get-tuple-element.157), channel_id=1, source_target_pairs={{1,0},{2,1},{3,2},{4,3},{5,4},{6,5},{7,6},{9,8},{10,9},{11,10},{12... | collective-permute-start | bytes 21896 | tf_op jit(solution)/shard_map/ppermute | solution.py:28
  17.2 2.2 collective-permute-start.2
  20.9 3.3 %collective-permute-done.2 = bf16[2,152,12]{2,1,0:T(8,128)(2,1)S(1)} collective-permute-done((bf16[2,152,12]{2,1,0:T(8,128)(2,1)S(1)}, bf16[2,152,12]{2,1,0:T(8,128)(2,1)S(1)}, u32[]{:S(2)}, u32[]{:S(2)}) %collective-permute-start.2) | collective-permute-done | bytes 7328 | tf_op jit(solution)/shard_map/ppermute | solution.py:26
  27.9 2.8 %collective-permute-start.4 = (bf16[32,256]{1,0:T(8,128)(2,1)S(1)}, bf16[32,256]{1,0:T(8,128)(2,1)S(1)}, u32[]{:S(2)}, u32[]{:S(2)}) collective-permute-start(bf16[32,256]{1,0:T(8,128)(2,1)S(1)} %get-tuple-element.163), channel_id=1, source_target_pairs={{0,8},{8,16},{16,24},{1,9},{9,17},{17,25},{2,10},{10,18},{18,26},{... | collective-permute-start | bytes 49160 | tf_op jit(solution)/shard_map/ppermute | solution.py:26
  32.7 3.1 %collective-permute-done.5 = bf16[32,256]{1,0:T(8,128)(2,1)S(1)} collective-permute-done((bf16[32,256]{1,0:T(8,128)(2,1)S(1)}, bf16[32,256]{1,0:T(8,128)(2,1)S(1)}, u32[]{:S(2)}, u32[]{:S(2)}) %collective-permute-start.5) | collective-permute-done | bytes 16416 | tf_op jit(solution)/shard_map/ppermute | solution.py:28
  37.8 3.4 %collective-permute-start.6 = (bf16[192,32]{1,0:T(8,128)(2,1)S(1)}, bf16[192,32]{1,0:T(8,128)(2,1)S(1)}, u32[]{:S(2)}, u32[]{:S(2)}) collective-permute-start(bf16[192,32]{1,0:T(8,128)(2,1)S(1)} %get-tuple-element.160), channel_id=1, source_target_pairs={{0,1},{1,2},{2,3},{3,4},{4,5},{5,6},{6,7},{8,9},{9,10},{10,11},{11... | collective-permute-start | bytes 36872 | tf_op jit(solution)/shard_map/ppermute | solution.py:26
  45.4 213.5 %while.13 = (s32[]{:T(128)}, f32[8,4096]{1,0:T(8,128)S(1)}, s32[]{:T(128)}, s32[]{:T(128)}, s32[8]{0:T(128)S(1)}, /*index=5*/bf16[8,16384]{1,0:T(8,128)(2,1)S(1)...) while((s32[]{:T(128)}, f32[8,4096]{1,0:T(8,128)S(1)}, s32[]{:T(128)}, s32[]{:T(128)}, ...), condition=%wide.region_9.11_spmd, body=%wide.region_5.10_spmd.sunk | while | flops 420100192 | bytes 62792896 | solution.py:161
  48.1 56.5 %gather_fusion.2 = bf16[8192,4,64]{2,1,0:T(4,128)(2,1)} fusion(bf16[4,64,128]{1,0,2:T(4,128)(2,1)S(1)} %pad.9.clone.2, s32[8192]{0:T(1024)S(1)} %fusion.323), kind=kCustom, calls=%fused_computation.4.clone.1 | custom fusion | bytes 8421376 | tf_op jit(solution)/shard_map/while/body/gather | solution.py:116
  104.6 10.1 %copy.125 = bf16[64,128,4,64]{1,0,3,2:T(8,128)(2,1)} copy(bf16[64,128,4,64]{3,2,1,0:T(4,128)(2,1)} %bitcast.144) | data formatting | bytes 8388608 | tf_op jit(solution)/shard_map/while/body/gather | solution.py:116
  115.4 28.5 %gather_fusion.4 = bf16[4096,4,128]{2,1,0:T(4,128)(2,1)} fusion(bf16[4,128,128]{2,0,1:T(4,128)(2,1)S(1)} %bitcast.143, s32[4096]{0:T(1024)S(1)} %broadcast_clamp_fusion.2), kind=kCustom, calls=%fused_computation.2.clone.1 | custom fusion | bytes 8404992 | tf_op jit(solution)/shard_map/while/body/gather | solution.py:113
  143.9 2.9 %copy.126 = bf16[4096,4,128]{2,0,1:T(8,128)(2,1)S(1)} copy(bf16[4096,4,128]{2,1,0:T(4,128)(2,1)} %gather_fusion.4) | data formatting | bytes 8388608 | tf_op jit(solution)/shard_map/while/body/gather | solution.py:113
  147.7 3.7 %fusion.326 = f32[4,64,64]{2,1,0:T(8,128)S(1)} fusion(bf16[64,128,4,64]{1,0,3,2:T(8,128)(2,1)S(1)} %copy-done, bf16[4,64,64,128]{3,2,1,0:T(8,128)(2,1)S(1)} %bitcast.146, f32[4,2,64,64]{3,2,0,1:T(8,128)S(1)} %fusion.325, f32[4]{0:T(128)S(1)} %multiply_reduce_fusion.2), kind=kOutput, calls=%fused_computation.13.clone.1 | convolution fusion | flops 268533760 | bytes 8585232 | tf_op jit(solution)/shard_map/while/body/gaiq,gidq->gad/dot_general | solution.py:117
  154.8 56.5 %gather_fusion.2 = bf16[8192,4,64]{2,1,0:T(4,128)(2,1)} fusion(bf16[4,64,128]{1,0,2:T(4,128)(2,1)S(1)} %pad.9.clone.2, s32[8192]{0:T(1024)S(1)} %fusion.323), kind=kCustom, calls=%fused_computation.4.clone.1 | custom fusion | bytes 8421376 | tf_op jit(solution)/shard_map/while/body/gather | solution.py:116
  211.2 10.1 %copy.125 = bf16[64,128,4,64]{1,0,3,2:T(8,128)(2,1)} copy(bf16[64,128,4,64]{3,2,1,0:T(4,128)(2,1)} %bitcast.144) | data formatting | bytes 8388608 | tf_op jit(solution)/shard_map/while/body/gather | solution.py:116
  222.1 28.5 %gather_fusion.4 = bf16[4096,4,128]{2,1,0:T(4,128)(2,1)} fusion(bf16[4,128,128]{2,0,1:T(4,128)(2,1)S(1)} %bitcast.143, s32[4096]{0:T(1024)S(1)} %broadcast_clamp_fusion.2), kind=kCustom, calls=%fused_computation.2.clone.1 | custom fusion | bytes 8404992 | tf_op jit(solution)/shard_map/while/body/gather | solution.py:113
  250.5 2.9 %copy.126 = bf16[4096,4,128]{2,0,1:T(8,128)(2,1)S(1)} copy(bf16[4096,4,128]{2,1,0:T(4,128)(2,1)} %gather_fusion.4) | data formatting | bytes 8388608 | tf_op jit(solution)/shard_map/while/body/gather | solution.py:113
  254.4 3.7 %fusion.326 = f32[4,64,64]{2,1,0:T(8,128)S(1)} fusion(bf16[64,128,4,64]{1,0,3,2:T(8,128)(2,1)S(1)} %copy-done, bf16[4,64,64,128]{3,2,1,0:T(8,128)(2,1)S(1)} %bitcast.146, f32[4,2,64,64]{3,2,0,1:T(8,128)S(1)} %fusion.325, f32[4]{0:T(128)S(1)} %multiply_reduce_fusion.2), kind=kOutput, calls=%fused_computation.13.clone.1 | convolution fusion | flops 268533760 | bytes 8585232 | tf_op jit(solution)/shard_map/while/body/gaiq,gidq->gad/dot_general | solution.py:117
  259.8 21.1 %while.14 = (s32[]{:T(128)}, f32[8,64,64]{2,1,0:T(8,128)S(1)}, s32[8,3]{0,1:T(4,128)S(1)}, f32[8,8,8]{2,1,0:T(8,128)S(1)}, s32[]{:T(128)}) while((s32[]{:T(128)}, f32[8,64,64]{2,1,0:T(8,128)S(1)}, s32[8,3]{0,1:T(4,128)S(1)}, f32[8,8,8]{2,1,0:T(8,128)S(1)}, s32[]{:T(128)}) %tuple.88), condition=%wide.while_cond, body=%wide.while_body.sunk | while | flops 2 | bytes 8329 | solution.py:170
  260.5 2.0 dynamic-slice_dynamic-update-slice_fusion.2
  263.1 2.0 dynamic-slice_dynamic-update-slice_fusion.2
  265.7 2.0 dynamic-slice_dynamic-update-slice_fusion.2
  268.4 2.0 dynamic-slice_dynamic-update-slice_fusion.2
  (171 shorter events, 45.6 us)
Async XLA Ops:
  1.4 11.7 %collective-permute-start.1 = (bf16[2,12,256]{2,1,0:T(8,128)(2,1)S(1)}, bf16[2,12,256]{2,1,0:T(8,128)(2,1)S(1)}, u32[]{:S(2)}, u32[]{:S(2)}) collective-permute-start(bf16[2,12,256]{2,1,0:T(8,128)(2,1)S(1)} %get-tuple-element.159), channel_id=1, source_target_pairs={{8,0},{16,8},{24,16},{9,1},{17,9},{25,17},{10,2},{18,10},{26,18},{... | collective-permute-start | bytes 36872 | tf_op jit(solution)/shard_map/ppermute | solution.py:28
  4.0 9.1 %collective-permute-start = (bf16[2,12,256]{2,1,0:T(8,128)(2,1)S(1)}, bf16[2,12,256]{2,1,0:T(8,128)(2,1)S(1)}, u32[]{:S(2)}, u32[]{:S(2)}) collective-permute-start(bf16[2,12,256]{2,1,0:T(8,128)(2,1)S(1)} %get-tuple-element.158), channel_id=1, source_target_pairs={{0,8},{8,16},{16,24},{1,9},{9,17},{17,25},{2,10},{10,18},{18,26},{... | collective-permute-start | bytes 36872 | tf_op jit(solution)/shard_map/ppermute | solution.py:26
  14.1 6.7 %collective-permute-start.3 = (bf16[2,152,12]{2,1,0:T(8,128)(2,1)S(1)}, bf16[2,152,12]{2,1,0:T(8,128)(2,1)S(1)}, u32[]{:S(2)}, u32[]{:S(2)}) collective-permute-start(bf16[2,152,12]{2,1,0:T(8,128)(2,1)S(1)} %get-tuple-element.157), channel_id=1, source_target_pairs={{1,0},{2,1},{3,2},{4,3},{5,4},{6,5},{7,6},{9,8},{10,9},{11,10},{12... | collective-permute-start | bytes 21896 | tf_op jit(solution)/shard_map/ppermute | solution.py:28
  17.2 7.0 %collective-permute-start.2 = (bf16[2,152,12]{2,1,0:T(8,128)(2,1)S(1)}, bf16[2,152,12]{2,1,0:T(8,128)(2,1)S(1)}, u32[]{:S(2)}, u32[]{:S(2)}) collective-permute-start(bf16[2,152,12]{2,1,0:T(8,128)(2,1)S(1)} %get-tuple-element.156), channel_id=1, source_target_pairs={{0,1},{1,2},{2,3},{3,4},{4,5},{5,6},{6,7},{8,9},{9,10},{10,11},{11... | collective-permute-start | bytes 21896 | tf_op jit(solution)/shard_map/ppermute | solution.py:26
  25.8 15.4 %copy-start.1 = (s32[2,4]{1,0:T(2,128)S(1)}, s32[2,4]{1,0:T(2,128)}, u32[]{:S(2)}) copy-start(s32[2,4]{1,0:T(2,128)} %param.14) | copy-start | bytes 100
  27.9 4.8 %collective-permute-start.4 = (bf16[32,256]{1,0:T(8,128)(2,1)S(1)}, bf16[32,256]{1,0:T(8,128)(2,1)S(1)}, u32[]{:S(2)}, u32[]{:S(2)}) collective-permute-start(bf16[32,256]{1,0:T(8,128)(2,1)S(1)} %get-tuple-element.163), channel_id=1, source_target_pairs={{0,8},{8,16},{16,24},{1,9},{9,17},{17,25},{2,10},{10,18},{18,26},{... | collective-permute-start | bytes 49160 | tf_op jit(solution)/shard_map/ppermute | solution.py:26
  30.7 5.1 %collective-permute-start.5 = (bf16[32,256]{1,0:T(8,128)(2,1)S(1)}, bf16[32,256]{1,0:T(8,128)(2,1)S(1)}, u32[]{:S(2)}, u32[]{:S(2)}) collective-permute-start(bf16[32,256]{1,0:T(8,128)(2,1)S(1)} %get-tuple-element.162), channel_id=1, source_target_pairs={{8,0},{16,8},{24,16},{9,1},{17,9},{25,17},{10,2},{18,10},{26,18},{... | collective-permute-start | bytes 49160 | tf_op jit(solution)/shard_map/ppermute | solution.py:28
  35.9 7.0 %collective-permute-start.7 = (bf16[192,32]{1,0:T(8,128)(2,1)S(1)}, bf16[192,32]{1,0:T(8,128)(2,1)S(1)}, u32[]{:S(2)}, u32[]{:S(2)}) collective-permute-start(bf16[192,32]{1,0:T(8,128)(2,1)S(1)} %get-tuple-element.161), channel_id=1, source_target_pairs={{1,0},{2,1},{3,2},{4,3},{5,4},{6,5},{7,6},{9,8},{10,9},{11,10},{12... | collective-permute-start | bytes 36872 | tf_op jit(solution)/shard_map/ppermute | solution.py:28
  37.8 5.7 %collective-permute-start.6 = (bf16[192,32]{1,0:T(8,128)(2,1)S(1)}, bf16[192,32]{1,0:T(8,128)(2,1)S(1)}, u32[]{:S(2)}, u32[]{:S(2)}) collective-permute-start(bf16[192,32]{1,0:T(8,128)(2,1)S(1)} %get-tuple-element.160), channel_id=1, source_target_pairs={{0,1},{1,2},{2,3},{3,4},{4,5},{5,6},{6,7},{8,9},{9,10},{10,11},{11... | collective-permute-start | bytes 36872 | tf_op jit(solution)/shard_map/ppermute | solution.py:26
  143.8 3.9 %copy-start = (bf16[64,128,4,64]{1,0,3,2:T(8,128)(2,1)S(1)}, bf16[64,128,4,64]{1,0,3,2:T(8,128)(2,1)}, u32[]{:S(2)}) copy-start(bf16[64,128,4,64]{1,0,3,2:T(8,128)(2,1)} %copy.125) | copy-start | bytes 12582916 | tf_op jit(solution)/shard_map/while
  250.5 3.9 %copy-start = (bf16[64,128,4,64]{1,0,3,2:T(8,128)(2,1)S(1)}, bf16[64,128,4,64]{1,0,3,2:T(8,128)(2,1)}, u32[]{:S(2)}) copy-start(bf16[64,128,4,64]{1,0,3,2:T(8,128)(2,1)} %copy.125) | copy-start | bytes 12582916 | tf_op jit(solution)/shard_map/while
where the time goes:
time: 283 us; the launch traced here: 282 us
  local copies, waits for them, and re-layouts  233 us (82%)
  starting transfers between devices  20.9 us (7%)
  matrix products  10.3 us (4%)
  other arithmetic  9.17 us (3%)
  waiting for transfers between devices  7.13 us (3%)
    gather x4, local copies, waits for them, and re-layouts, surfaces(): spread[:, :, jnp.where((column_gap >= 0) & (column_gap < CHIP), column_ga...  133 us
    gather x4, local copies, waits for them, and re-layouts, surfaces(): hankel = window[:, lag_index[:, None] + lag_index[None, :], :]  62.7 us
    gather x24, local copies, waits for them, and re-layouts  21.1 us
    ppermute x4, starting transfers between devices, padded_2(): lax.ppermute(tail, axis, [(i, (i + 1) % count) for i in range(ends)])  11.5 us
    ppermute x4, starting transfers between devices, padded_2(): lax.ppermute(head, axis, [((i + 1) % count, i) for i in range(ends)])  9.45 us
    dot_general x2, matrix products, surfaces(): jnp.einsum('gaiq,gidq->gad', hankel, toeplitz, preferred_element_type=jnp...  7.42 us
  transfers between devices with their start and end apart: 8, of which 3 were waited for; matrix products, arithmetic and copies ran while one was open for 3% of the time, Pallas kernels for 0%

commit v1 on v0

v1 whole, which is shorter than its diff:
```python
import jax
import jax.numpy as jnp
import ml_dtypes
import numpy as np
from jax import lax
from jax.experimental import pallas as pl
from jax.experimental.pallas import tpu as pltpu
from jax.sharding import PartitionSpec as P

CHIP = 64
SEARCH = 32
TAPS = 8
NBIN = 16
OVERS = 16
PATCH = 8
LINES = 48
COLS = 128
GROUP = 8
EPSILON = 1e-06
F32, BF16 = jnp.float32, jnp.bfloat16


def lanczos(x):
    return np.where(np.abs(x) < 4, np.sinc(x) * np.sinc(x / 4), 0.0)


def tap_table():
    taps = lanczos(np.arange(TAPS)[None, :] - 3 - np.arange(NBIN)[:, None] / NBIN)
    taps = taps.astype(np.float32).astype(ml_dtypes.bfloat16).astype(np.float32)
    return np.concatenate([np.zeros((1, TAPS), np.float32), taps]).reshape(-1)


def lobe_table():
    at = (np.arange(2 * OVERS) - OVERS) / OVERS
    lobes = lanczos(at[:, None] - (np.arange(PATCH) - (PATCH // 2 - 1))[None, :])
    return np.pad(lobes.astype(np.float32), ((0, 0), (0, 128 - PATCH)))


def with_halo(cells, axis, dim, width):
    count = lax.axis_size(axis)
    head = lax.slice_in_dim(cells, 0, width, axis=dim)
    tail = lax.slice_in_dim(cells, cells.shape[dim] - width, cells.shape[dim], axis=dim)
    up = [(i, i + 1) for i in range(count - 1)]
    down = [(i + 1, i) for i in range(count - 1)]
    return jnp.concatenate(
        [lax.ppermute(tail, axis, up), cells, lax.ppermute(head, axis, down)], axis=dim
    )


def dot_nt(a, b, **kw):
    return lax.dot_general(a, b, (((1,), (1,)), ((), ())), preferred_element_type=F32, **kw)


def split3(x):
    hi = x.astype(BF16)
    rest = x - hi.astype(F32)
    mid = rest.astype(BF16)
    return hi, mid, (rest - mid.astype(F32)).astype(BF16)


def band(rows, span, base, tab, par, shift_at, bin_at):
    gap = lax.broadcasted_iota(jnp.int32, (rows, span), 1) - lax.broadcasted_iota(
        jnp.int32, (rows, span), 0
    )
    gap = gap - (base - (TAPS // 2 - 1) + par[shift_at])
    f = par[bin_at]
    out = jnp.zeros((rows, span), F32)
    for t in range(TAPS):
        out = jnp.where(gap == t, tab[f * TAPS + t], out)
    return out.astype(BF16)


def body(
    nu, nv, par, tab, mask, peaks, ext, ref, lobes, out, patch, amp, win, cen, wts, toep, tmp, tmp2,
    flat, flat2,
):
    chunks = (nv * CHIP + 2 * SEARCH + 127) // 128
    mu, mv = nu + 2, nv + 2
    for u in range(-1, nu + 1):
        rows = CHIP if 0 <= u < nu else SEARCH
        first = u * CHIP + (CHIP - SEARCH if u < 0 else 0)
        low = (first + LINES - 12) // 16 * 16
        high = min(-(-(first + LINES + rows + 12) // 16) * 16, nu * CHIP + 2 * LINES)
        totals = [None] * chunks
        for v in range(-1, nv + 1):
            at = (u + 1) * mv + v + 1
            begin = max(v * CHIP, -SEARCH)
            end = min(v * CHIP + CHIP, nv * CHIP + SEARCH)
            left = (begin + COLS - 12) // 128 * 128
            right = left + 256
            a = band(rows, high - low, first + LINES - low, tab, par, at, 2 * mu * mv + at)
            half = jnp.concatenate(
                [
                    jnp.dot(a, ext[c, low:high, left:right], preferred_element_type=F32)
                    for c in range(2)
                ],
                axis=0,
            ).astype(BF16)
            b = band(
                end - begin, 256, begin + COLS - left, tab, par, mu * mv + at, 3 * mu * mv + at
            )
            spot = begin + SEARCH
            while spot < end + SEARCH:
                m = spot // 128
                stop = min(end + SEARCH, (m + 1) * 128)
                part = b[spot - SEARCH - begin : stop - SEARCH - begin]
                pieces = [part]
                if spot > m * 128:
                    pieces.insert(0, jnp.zeros((spot - m * 128, 256), BF16))
                if stop < m * 128 + 128:
                    pieces.append(jnp.zeros((m * 128 + 128 - stop, 256), BF16))
                piece = jnp.concatenate(pieces, axis=0) if len(pieces) > 1 else part
                term = dot_nt(half, piece)
                totals[m] = term if totals[m] is None else totals[m] + term
                spot = stop
        for m in range(chunks):
            re, im = totals[m][:rows], totals[m][rows:]
            amp[first + SEARCH : first + SEARCH + rows, m * 128 : m * 128 + 128] = (
                jnp.sqrt(re * re + im * im).astype(BF16).astype(F32)
            )

    lane = lax.broadcasted_iota(jnp.int32, (2 * CHIP, 128), 1)
    low_lanes = lane < CHIP
    re = ref[0].astype(F32)
    im = ref[1].astype(F32)
    across = jnp.sqrt(re * re + im * im).astype(BF16).astype(F32).T
    for u in range(nu):
        for v in range(nv):
            n = u * nv + v
            lines = slice(u * CHIP, u * CHIP + 2 * CHIP)
            m = v // 2
            if v % 2 == 0:
                win[n] = amp[lines, m * 128 : m * 128 + 128]
            else:
                win[n] = jnp.where(
                    low_lanes,
                    pltpu.roll(amp[lines, m * 128 : m * 128 + 128], 64, 1),
                    pltpu.roll(amp[lines, m * 128 + 128 : m * 128 + 256], 64, 1),
                )
            wide = u // 2 * 128
            chip = across[v * CHIP : v * CHIP + CHIP, wide : wide + 128]
            if u % 2:
                chip = pltpu.roll(chip, 64, 1)
            keep = low_lanes[:CHIP]
            chip = jnp.where(keep, chip, 0.0)
            mean = jnp.sum(jnp.sum(chip, axis=1, keepdims=True), axis=0, keepdims=True)
            mean = mean * (1.0 / (CHIP * CHIP))
            cen[n] = jnp.where(keep, (chip - mean).astype(BF16).astype(F32), 0.0)

    gap_r = lax.broadcasted_iota(jnp.int32, (CHIP, 128), 1) - lax.broadcasted_iota(
        jnp.int32, (CHIP, 128), 0
    )
    ones_r = jnp.where((gap_r >= 0) & (gap_r < CHIP), 1.0, 0.0).astype(BF16)
    gap_c = lax.broadcasted_iota(jnp.int32, (128, 128), 0) - lane
    ones_c = jnp.where((gap_c >= 0) & (gap_c < CHIP), 1.0, 0.0).astype(BF16)

    def one_chip(n, carry):
        w = win[n]
        for s in range(GROUP):
            shifted = pltpu.roll(w, 128 - s, 1) if s else w
            wts[s * 128 : s * 128 + 128, :] = shifted.astype(BF16)
        centred = cen[n]
        for j in range(CHIP):
            k, s = j // GROUP, j % GROUP
            line = jnp.broadcast_to(centred[j : j + 1, :], (CHIP, 128))
            toep[k * CHIP : k * CHIP + CHIP, s * 128 : s * 128 + 128] = pltpu.roll(
                line, 0, 1, stride=1, stride_axis=0
            ).astype(BF16)
        prod = jnp.dot(toep[...], wts[...], preferred_element_type=F32)
        cross = prod[:CHIP]
        for k in range(1, CHIP // GROUP):
            cross = cross + pltpu.roll(prod[k * CHIP : k * CHIP + CHIP], 128 - k * GROUP, 1)
        energy = jnp.sum(jnp.sum(centred * centred, axis=1, keepdims=True), axis=0, keepdims=True)
        square = w * w
        square_hi = square.astype(BF16)
        square_lo = (square - square_hi.astype(F32)).astype(BF16)
        sums = jnp.dot(
            ones_r,
            jnp.concatenate([w.astype(BF16), square_hi, square_lo], axis=1),
            preferred_element_type=F32,
        )
        terms = split3(sums[:, :128]) + split3(sums[:, 128:256] + sums[:, 256:])
        boxes = jnp.dot(jnp.concatenate(terms, axis=0), ones_c, preferred_element_type=F32)
        box = [boxes[i * CHIP : i * CHIP + CHIP] for i in range(6)]
        total = box[2] + box[1] + box[0]
        squares = box[5] + box[4] + box[3]
        normed = cross / jnp.sqrt(
            energy * (squares - total * total * (1.0 / (CHIP * CHIP))) + EPSILON
        )
        land = (mask[n] == 1) & low_lanes[:CHIP]
        surface = jnp.where(land, normed, 0.0)
        tmp[...] = surface
        pairs = tmp[pl.ds(0, 32, stride=2), :] + pltpu.roll(tmp[pl.ds(1, 32, stride=2), :], 64, 1)
        flat[n] = pairs
        lead = SEARCH - (PATCH // 2 - 1)
        lobe_a = pltpu.roll(lobes[...], peaks[n] + lead, 1)
        lobe_d = pltpu.roll(lobes[...], peaks[nu * nv + n] + lead, 1)
        near = jnp.dot(
            lobe_a,
            jnp.concatenate([surface, jnp.zeros((CHIP, 128), F32)], axis=0),
            preferred_element_type=F32,
            precision=lax.Precision.HIGHEST,
        )
        tall = jnp.concatenate([lobe_d, jnp.zeros((96, 128), F32)], axis=0)
        tmp2[...] = dot_nt(near, tall, precision=lax.Precision.HIGHEST)
        quads = tmp2[pl.ds(0, 8, stride=4), :]
        for r in range(1, 4):
            quads = quads + pltpu.roll(tmp2[pl.ds(r, 8, stride=4), :], 32 * r, 1)
        flat2[n] = quads
        return carry

    lax.fori_loop(0, nu * nv, one_chip, 0)
    for u in range(nu):
        for v in range(nv):
            for m in range(CHIP // 2):
                out[u, v : v + 1, m * 128 : m * 128 + 128] = flat[u * nv + v, m : m + 1, :]
            for m in range(8):
                patch[u, v : v + 1, m * 128 : m * 128 + 128] = flat2[u * nv + v, m : m + 1, :]


def per_device(reference_image, secondary_image, block_shifts, shift_bins, land_mask, coarse_peaks):
    nu, nv = land_mask.shape
    par = jnp.concatenate([block_shifts, shift_bins + 1], axis=0)
    par = with_halo(with_halo(par, "az", 1, 1), "rg", 2, 1)
    ext = with_halo(with_halo(secondary_image, "az", 1, LINES), "rg", 2, COLS)
    smem = pl.BlockSpec(memory_space=pltpu.SMEM)
    vmem = pl.BlockSpec(memory_space=pltpu.VMEM)
    n = nu * nv
    chunks = (nv * CHIP + 2 * SEARCH + 127) // 128

    def kernel(*refs):
        body(nu, nv, *refs)

    return pl.pallas_call(
        kernel,
        out_shape=(
            jax.ShapeDtypeStruct((nu, nv, CHIP * CHIP), F32),
            jax.ShapeDtypeStruct((nu, nv, 4 * OVERS * OVERS), F32),
        ),
        in_specs=[smem] * 4 + [vmem] * 3,
        out_specs=(vmem, vmem),
        scratch_shapes=[
            pltpu.VMEM((nu * CHIP + 2 * SEARCH, chunks * 128), F32),
            pltpu.VMEM((n, 2 * CHIP, 128), F32),
            pltpu.VMEM((n, CHIP, 128), F32),
            pltpu.VMEM((GROUP * 128, 128), BF16),
            pltpu.VMEM((CHIP * CHIP // GROUP, GROUP * 128), BF16),
            pltpu.VMEM((CHIP, 128), F32),
            pltpu.VMEM((2 * OVERS, 128), F32),
            pltpu.VMEM((n, CHIP // 2, 128), F32),
            pltpu.VMEM((n, 8, 128), F32),
        ],
        compiler_params=pltpu.CompilerParams(vmem_limit_bytes=48 * 1024 * 1024),
    )(
        par.reshape(-1),
        jnp.asarray(tap_table()),
        land_mask.reshape(-1),
        coarse_peaks.reshape(-1),
        ext,
        reference_image,
        jnp.asarray(lobe_table()),
    )


def solution(mesh):
    cut = P(None, "az", "rg")
    return jax.shard_map(
        per_device,
        mesh=mesh,
        in_specs=(cut, cut, cut, cut, P("az", "rg"), cut),
        out_specs=(P("az", "rg", None), P("az", "rg", None)),
        check_vma=False,
    )
```

time: 283 us -> 46.3 us (0.16)
  the two profiles are of different devices: /device:TPU:25 before, /device:TPU:14 now
where the time goes in v1:
time: 46.3 us; the launch traced here: 45.9 us
  starting transfers between devices  23.5 us (51%)
  Pallas kernels  12.7 us (27%)
  waiting for transfers between devices  5.99 us (13%)
  local copies, waits for them, and re-layouts  2.06 us (4%)
  other arithmetic  0.84 us (2%)
  between operations  0.84 us (2%)
    pallas_call x1, Pallas kernels, per_device(): pl.pallas_call(kernel, out_shape=(jax.ShapeDtypeStruct((nu, nv, CHIP * CH...  12.7 us
    ppermute x4, starting transfers between devices, with_halo(): lax.ppermute(head, axis, down)  11.8 us
    ppermute x4, starting transfers between devices, with_halo(): lax.ppermute(tail, axis, up)  11.7 us
    ppermute x4, waiting for transfers between devices, with_halo(): lax.ppermute(head, axis, down)  5.98 us
  transfers between devices with their start and end apart: 8, of which 2 were waited for; matrix products, arithmetic and copies ran while one was open for 3% of the time, Pallas kernels for 0%

profile of v1, /device:TPU:14, one launch (start us, length us, event | category | flops | bytes accessed | tf_op | source)
XLA Modules:
  0.0 45.9 jit_solution(10263611729053488375)
XLA Ops:
  0.6 0.7 %broadcast_add_fusion = s32[2,2,4]{2,1,0:T(2,128)S(1)} fusion(s32[2,2,4]{2,1,0:T(2,128)} %param.11), kind=kLoop, calls=%fused_computation.10 | loop fusion | flops 16 | bytes 128 | tf_op jit(solution)/shard_map/add | solution.py:223
  1.3 1.9 %collective-permute-start = (s32[4,1,4]{2,1,0:T(1,128)S(1)}, s32[4,1,4]{2,1,0:T(1,128)S(1)}, u32[]{:S(2)}, u32[]{:S(2)}) collective-permute-start(s32[4,1,4]{2,1,0:T(1,128)S(1)} %get-tuple-element.8), channel_id=1, source_target_pairs={{0,8},{8,16},{16,24},{1,9},{9,17},{17,25},{2,10},{10,18},{18,26},{... | collective-permute-start | bytes 200 | tf_op jit(solution)/shard_map/ppermute | solution.py:46
  3.3 0.0 copy-start.3
  3.3 3.8 %collective-permute-start.1 = (s32[4,1,4]{2,1,0:T(1,128)S(1)}, s32[4,1,4]{2,1,0:T(1,128)S(1)}, u32[]{:S(2)}, u32[]{:S(2)}) collective-permute-start(s32[4,1,4]{2,1,0:T(1,128)S(1)} %get-tuple-element.9), channel_id=1, source_target_pairs={{8,0},{16,8},{24,16},{9,1},{17,9},{25,17},{10,2},{18,10},{26,18},{... | collective-permute-start | bytes 200 | tf_op jit(solution)/shard_map/ppermute | solution.py:46
  7.1 0.8 %fusion.2 = (bf16[2,48,256]{2,1,0:T(8,128)(2,1)S(1)}, bf16[2,48,256]{2,1,0:T(8,128)(2,1)S(1)}) fusion(bf16[2,128,256]{2,1,0:T(8,128)(2,1)} %param.9), kind=kLoop, calls=%fused_computation.12 | loop fusion | bytes 196608 | tf_op jit(solution)/shard_map/slice | solution.py:41
  7.9 2.1 %collective-permute-start.4 = (bf16[2,48,256]{2,1,0:T(8,128)(2,1)S(1)}, bf16[2,48,256]{2,1,0:T(8,128)(2,1)S(1)}, u32[]{:S(2)}, u32[]{:S(2)}) collective-permute-start(bf16[2,48,256]{2,1,0:T(8,128)(2,1)S(1)} %get-tuple-element.5), channel_id=1, source_target_pairs={{0,8},{8,16},{16,24},{1,9},{9,17},{17,25},{2,10},{10,18},{18,26},{... | collective-permute-start | bytes 147464 | tf_op jit(solution)/shard_map/ppermute | solution.py:46
  10.0 3.6 %collective-permute-start.5 = (bf16[2,48,256]{2,1,0:T(8,128)(2,1)S(1)}, bf16[2,48,256]{2,1,0:T(8,128)(2,1)S(1)}, u32[]{:S(2)}, u32[]{:S(2)}) collective-permute-start(bf16[2,48,256]{2,1,0:T(8,128)(2,1)S(1)} %get-tuple-element.4), channel_id=1, source_target_pairs={{8,0},{16,8},{24,16},{9,1},{17,9},{25,17},{10,2},{18,10},{26,18},{... | collective-permute-start | bytes 147464 | tf_op jit(solution)/shard_map/ppermute | solution.py:46
  13.6 0.1 reshape.14.refs_2_
  13.7 0.1 reshape.15.refs_3_
  13.9 1.5 %collective-permute-done.5 = bf16[2,48,256]{2,1,0:T(8,128)(2,1)S(1)} collective-permute-done((bf16[2,48,256]{2,1,0:T(8,128)(2,1)S(1)}, bf16[2,48,256]{2,1,0:T(8,128)(2,1)S(1)}, u32[]{:S(2)}, u32[]{:S(2)}) %collective-permute-start.5) | collective-permute-done | bytes 49184 | tf_op jit(solution)/shard_map/ppermute | solution.py:46
  15.4 3.4 %collective-permute-start.6 = (bf16[2,224,128]{2,1,0:T(8,128)(2,1)S(1)}, bf16[2,224,128]{2,1,0:T(8,128)(2,1)S(1)}, u32[]{:S(2)}, u32[]{:S(2)}) collective-permute-start(bf16[2,224,128]{2,1,0:T(8,128)(2,1)S(1)} %get-tuple-element.2), channel_id=1, source_target_pairs={{0,1},{1,2},{2,3},{3,4},{4,5},{5,6},{6,7},{8,9},{9,10},{10,11},{11... | collective-permute-start | bytes 344072 | tf_op jit(solution)/shard_map/ppermute | solution.py:46
  18.8 2.4 %collective-permute-start.7 = (bf16[2,224,128]{2,1,0:T(8,128)(2,1)S(1)}, bf16[2,224,128]{2,1,0:T(8,128)(2,1)S(1)}, u32[]{:S(2)}, u32[]{:S(2)}) collective-permute-start(bf16[2,224,128]{2,1,0:T(8,128)(2,1)S(1)} %get-tuple-element.3), channel_id=1, source_target_pairs={{1,0},{2,1},{3,2},{4,3},{5,4},{6,5},{7,6},{9,8},{10,9},{11,10},{12... | collective-permute-start | bytes 344072 | tf_op jit(solution)/shard_map/ppermute | solution.py:46
  21.3 0.1 fusion.3
  21.3 4.3 %collective-permute-start.2 = (s32[4,4,1]{2,1,0:T(4,128)S(1)}, s32[4,4,1]{2,1,0:T(4,128)S(1)}, u32[]{:S(2)}, u32[]{:S(2)}) collective-permute-start(s32[4,4,1]{2,1,0:T(4,128)S(1)} %get-tuple-element.6), channel_id=1, source_target_pairs={{0,1},{1,2},{2,3},{3,4},{4,5},{5,6},{6,7},{8,9},{9,10},{10,11},{11... | collective-permute-start | bytes 200 | tf_op jit(solution)/shard_map/ppermute | solution.py:46
  25.7 1.9 %collective-permute-start.3 = (s32[4,4,1]{2,1,0:T(4,128)S(1)}, s32[4,4,1]{2,1,0:T(4,128)S(1)}, u32[]{:S(2)}, u32[]{:S(2)}) collective-permute-start(s32[4,4,1]{2,1,0:T(4,128)S(1)} %get-tuple-element.7), channel_id=1, source_target_pairs={{1,0},{2,1},{3,2},{4,3},{5,4},{6,5},{7,6},{9,8},{10,9},{11,10},{12... | collective-permute-start | bytes 200 | tf_op jit(solution)/shard_map/ppermute | solution.py:46
  27.6 4.5 %collective-permute-done.3 = s32[4,4,1]{2,1,0:T(4,128)S(1)} collective-permute-done((s32[4,4,1]{2,1,0:T(4,128)S(1)}, s32[4,4,1]{2,1,0:T(4,128)S(1)}, u32[]{:S(2)}, u32[]{:S(2)}) %collective-permute-start.3) | collective-permute-done | bytes 96 | tf_op jit(solution)/shard_map/ppermute | solution.py:46
  32.1 0.1 pad_add_fusion.1
  32.2 0.1 reshape.13.refs_0_
  32.3 0.0 copy-start
  32.3 0.0 copy-start.1
  32.3 0.0 copy-start.2
  32.4 0.1 pad_maximum_fusion.refs_4_
  32.4 0.8 %copy-done = bf16[2,128,256]{2,1,0:T(8,128)(2,1)S(1)} copy-done((bf16[2,128,256]{2,1,0:T(8,128)(2,1)S(1)}, bf16[2,128,256]{2,1,0:T(8,128)(2,1)}, u32[]{:S(2)}) %copy-start) | copy-done | bytes 131096
  33.2 12.7 %shard_map.95 = (f32[2,4,4096]{2,1,0:T(4,128)}, f32[2,4,1024]{2,1,0:T(4,128)}) custom-call(s32[96]{0:T(128)S(1)} %reshape.13.refs_0_, f32[136]{0:T(256)S(1)} %copy-done.2, s32[8]{0:T(128)S(1)} %reshape.14.refs_2_, s32[16]{0:T(128)S(1)} %reshape.15.refs_3_, bf16[2,224,512]{2,1,0:T(8,128)(2,1)S(1)} %pad_maximum_fusion.refs_4_, ...), custom_call_target="tpu_custom_call" | custom-call | tf_op jit(solution)/shard_map/pallas_call | solution.py:234
  (21 shorter events, 0.1 us)
Async XLA Ops:
  0.6 0.7 %copy-start.4 = (s32[2,2,4]{2,1,0:T(2,128)S(1)}, s32[2,2,4]{2,1,0:T(2,128)}, u32[]{:S(2)}) copy-start(s32[2,2,4]{2,1,0:T(2,128)} %param.10) | copy-start | bytes 196
  1.3 12.5 %collective-permute-start = (s32[4,1,4]{2,1,0:T(1,128)S(1)}, s32[4,1,4]{2,1,0:T(1,128)S(1)}, u32[]{:S(2)}, u32[]{:S(2)}) collective-permute-start(s32[4,1,4]{2,1,0:T(1,128)S(1)} %get-tuple-element.8), channel_id=1, source_target_pairs={{0,8},{8,16},{16,24},{1,9},{9,17},{17,25},{2,10},{10,18},{18,26},{... | collective-permute-start | bytes 200 | tf_op jit(solution)/shard_map/ppermute | solution.py:46
  3.3 10.6 %copy-start.3 = (bf16[2,128,256]{2,1,0:T(8,128)(2,1)S(1)}, bf16[2,128,256]{2,1,0:T(8,128)(2,1)}, u32[]{:S(2)}) copy-start(bf16[2,128,256]{2,1,0:T(8,128)(2,1)} %param.9) | copy-start | bytes 393220
  3.3 10.5 %collective-permute-start.1 = (s32[4,1,4]{2,1,0:T(1,128)S(1)}, s32[4,1,4]{2,1,0:T(1,128)S(1)}, u32[]{:S(2)}, u32[]{:S(2)}) collective-permute-start(s32[4,1,4]{2,1,0:T(1,128)S(1)} %get-tuple-element.9), channel_id=1, source_target_pairs={{8,0},{16,8},{24,16},{9,1},{17,9},{25,17},{10,2},{18,10},{26,18},{... | collective-permute-start | bytes 200 | tf_op jit(solution)/shard_map/ppermute | solution.py:46
  7.9 5.7 %copy-start.6 = (s32[2,4]{1,0:T(2,128)S(1)}, s32[2,4]{1,0:T(2,128)}, u32[]{:S(2)}) copy-start(s32[2,4]{1,0:T(2,128)} %param.12) | copy-start | bytes 100
  7.9 5.8 %copy-start.5 = (s32[2,2,4]{2,1,0:T(2,128)S(1)}, s32[2,2,4]{2,1,0:T(2,128)}, u32[]{:S(2)}) copy-start(s32[2,2,4]{2,1,0:T(2,128)} %param.13) | copy-start | bytes 196
  7.9 5.9 %collective-permute-start.4 = (bf16[2,48,256]{2,1,0:T(8,128)(2,1)S(1)}, bf16[2,48,256]{2,1,0:T(8,128)(2,1)S(1)}, u32[]{:S(2)}, u32[]{:S(2)}) collective-permute-start(bf16[2,48,256]{2,1,0:T(8,128)(2,1)S(1)} %get-tuple-element.5), channel_id=1, source_target_pairs={{0,8},{8,16},{16,24},{1,9},{9,17},{17,25},{2,10},{10,18},{18,26},{... | collective-permute-start | bytes 147464 | tf_op jit(solution)/shard_map/ppermute | solution.py:46
  10.0 5.4 %collective-permute-start.5 = (bf16[2,48,256]{2,1,0:T(8,128)(2,1)S(1)}, bf16[2,48,256]{2,1,0:T(8,128)(2,1)S(1)}, u32[]{:S(2)}, u32[]{:S(2)}) collective-permute-start(bf16[2,48,256]{2,1,0:T(8,128)(2,1)S(1)} %get-tuple-element.4), channel_id=1, source_target_pairs={{8,0},{16,8},{24,16},{9,1},{17,9},{25,17},{10,2},{18,10},{26,18},{... | collective-permute-start | bytes 147464 | tf_op jit(solution)/shard_map/ppermute | solution.py:46
  15.4 16.9 %collective-permute-start.6 = (bf16[2,224,128]{2,1,0:T(8,128)(2,1)S(1)}, bf16[2,224,128]{2,1,0:T(8,128)(2,1)S(1)}, u32[]{:S(2)}, u32[]{:S(2)}) collective-permute-start(bf16[2,224,128]{2,1,0:T(8,128)(2,1)S(1)} %get-tuple-element.2), channel_id=1, source_target_pairs={{0,1},{1,2},{2,3},{3,4},{4,5},{5,6},{6,7},{8,9},{9,10},{10,11},{11... | collective-permute-start | bytes 344072 | tf_op jit(solution)/shard_map/ppermute | solution.py:46
  18.8 13.5 %collective-permute-start.7 = (bf16[2,224,128]{2,1,0:T(8,128)(2,1)S(1)}, bf16[2,224,128]{2,1,0:T(8,128)(2,1)S(1)}, u32[]{:S(2)}, u32[]{:S(2)}) collective-permute-start(bf16[2,224,128]{2,1,0:T(8,128)(2,1)S(1)} %get-tuple-element.3), channel_id=1, source_target_pairs={{1,0},{2,1},{3,2},{4,3},{5,4},{6,5},{7,6},{9,8},{10,9},{11,10},{12... | collective-permute-start | bytes 344072 | tf_op jit(solution)/shard_map/ppermute | solution.py:46
  21.3 6.3 %collective-permute-start.2 = (s32[4,4,1]{2,1,0:T(4,128)S(1)}, s32[4,4,1]{2,1,0:T(4,128)S(1)}, u32[]{:S(2)}, u32[]{:S(2)}) collective-permute-start(s32[4,4,1]{2,1,0:T(4,128)S(1)} %get-tuple-element.6), channel_id=1, source_target_pairs={{0,1},{1,2},{2,3},{3,4},{4,5},{5,6},{6,7},{8,9},{9,10},{10,11},{11... | collective-permute-start | bytes 200 | tf_op jit(solution)/shard_map/ppermute | solution.py:46
  25.7 6.4 %collective-permute-start.3 = (s32[4,4,1]{2,1,0:T(4,128)S(1)}, s32[4,4,1]{2,1,0:T(4,128)S(1)}, u32[]{:S(2)}, u32[]{:S(2)}) collective-permute-start(s32[4,4,1]{2,1,0:T(4,128)S(1)} %get-tuple-element.7), channel_id=1, source_target_pairs={{1,0},{2,1},{3,2},{4,3},{5,4},{6,5},{7,6},{9,8},{10,9},{11,10},{12... | collective-permute-start | bytes 200 | tf_op jit(solution)/shard_map/ppermute | solution.py:46
  32.3 0.9 %copy-start = (bf16[2,128,256]{2,1,0:T(8,128)(2,1)S(1)}, bf16[2,128,256]{2,1,0:T(8,128)(2,1)}, u32[]{:S(2)}) copy-start(bf16[2,128,256]{2,1,0:T(8,128)(2,1)} %refs_5_.1) | copy-start | bytes 393220
  32.3 0.9 %copy-start.1 = (f32[32,128]{1,0:T(8,128)S(1)}, f32[32,128]{1,0:T(8,128)}, u32[]{:S(2)}) copy-start(f32[32,128]{1,0:T(8,128)} %constant.7.clone.refs_6_) | copy-start | bytes 49156
  32.3 0.9 %copy-start.2 = (f32[136]{0:T(256)S(1)}, f32[136]{0:T(256)}, u32[]{:S(2)}) copy-start(f32[136]{0:T(256)} %constant.6.clone.refs_1_) | copy-start | bytes 1636

commit v2 on v1

--- a/solution.py
+++ b/solution.py
@@ -36,15 +36,96 @@
     return np.pad(lobes.astype(np.float32), ((0, 0), (0, 128 - PATCH)))
 
 
-def with_halo(cells, axis, dim, width):
-    count = lax.axis_size(axis)
-    head = lax.slice_in_dim(cells, 0, width, axis=dim)
-    tail = lax.slice_in_dim(cells, cells.shape[dim] - width, cells.shape[dim], axis=dim)
-    up = [(i, i + 1) for i in range(count - 1)]
-    down = [(i + 1, i) for i in range(count - 1)]
-    return jnp.concatenate(
-        [lax.ppermute(tail, axis, up), cells, lax.ppermute(head, axis, down)], axis=dim
-    )
+SIDES = [(i, j) for i in (-1, 0, 1) for j in (-1, 0, 1) if (i, j) != (0, 0)]
+
+
+def exchange(axes, par, img, out_par, out, got_par, got, sems):
+    lines, cols = img.shape[1:]
+    here = [lax.axis_index(a) for a in axes]
+    count = [lax.axis_size(a) for a in axes]
+
+    def inside(i, j):
+        row, col = here[0] + i, here[1] + j
+        return (row >= 0) & (row < count[0]) & (col >= 0) & (col < count[1])
+
+    got[...] = jnp.zeros_like(got)
+    got_par[...] = jnp.zeros_like(got_par)
+    barrier = pltpu.get_barrier_semaphore()
+    for i, j in SIDES:
+
+        @pl.when(inside(i, j))
+        def _():
+            pl.semaphore_signal(
+                barrier,
+                inc=1,
+                device_id=(here[0] + i, here[1] + j),
+                device_id_type=pl.DeviceIdType.MESH,
+            )
+
+    tall, wide = (
+        1 + jnp.where(h > 0, 1, 0) + jnp.where(h < n - 1, 1, 0) for h, n in zip(here, count)
+    )
+    pl.semaphore_wait(barrier, tall * wide - 1)
+
+    def spans(step, size, width):
+        if step == 0:
+            return pl.ds(0, size), pl.ds(width, size)
+        if step == 1:
+            return pl.ds(size - width, width), pl.ds(0, width)
+        return pl.ds(0, width), pl.ds(width + size, width)
+
+    def copies(k, i, j):
+        src_l, dst_l = spans(i, lines, LINES)
+        src_c, dst_c = spans(j, cols, COLS)
+        where = dict(
+            device_id=(here[0] + i, here[1] + j), device_id_type=pl.DeviceIdType.MESH
+        )
+        slot = 3 * (1 - i) + 1 - j
+        return (
+            pltpu.make_async_remote_copy(
+                src_ref=img.at[:, src_l, src_c],
+                dst_ref=got.at[:, dst_l, dst_c],
+                send_sem=sems.at[0, k],
+                recv_sem=sems.at[1, k],
+                **where,
+            ),
+            pltpu.make_async_remote_copy(
+                src_ref=par,
+                dst_ref=got_par.at[slot],
+                send_sem=sems.at[2, k],
+                recv_sem=sems.at[3, k],
+                **where,
+            ),
+        )
+
+    for k, (i, j) in enumerate(SIDES):
+
+        @pl.when(inside(i, j))
+        def _():
+            for copy in copies(k, i, j):
+                copy.start()
+
+    out[:, LINES : LINES + lines, COLS : COLS + cols] = img[...]
+    out_par[4:5, :] = par[...]
+    for k, (i, j) in enumerate(SIDES):
+
+        @pl.when(inside(i, j))
+        def _():
+            for copy in copies(k, i, j):
+                copy.wait_send()
+
+        @pl.when(inside(-i, -j))
+        def _():
+            for copy in copies(k, i, j):
+                copy.wait_recv()
+
+    out[:, :LINES, :] = got[:, :LINES, :]
+    out[:, LINES + lines :, :] = got[:, LINES + lines :, :]
+    out[:, LINES : LINES + lines, :COLS] = got[:, LINES : LINES + lines, :COLS]
+    out[:, LINES : LINES + lines, COLS + cols :] = got[:, LINES : LINES + lines, COLS + cols :]
+    for slot in range(9):
+        if slot != 4:
+            out_par[slot : slot + 1, :] = got_par[slot]
 
 
 def dot_nt(a, b, **kw):
@@ -58,12 +139,11 @@
     return hi, mid, (rest - mid.astype(F32)).astype(BF16)
 
 
-def band(rows, span, base, tab, par, shift_at, bin_at):
+def band(rows, span, base, tab, shift, f):
     gap = lax.broadcasted_iota(jnp.int32, (rows, span), 1) - lax.broadcasted_iota(
         jnp.int32, (rows, span), 0
     )
-    gap = gap - (base - (TAPS // 2 - 1) + par[shift_at])
-    f = par[bin_at]
+    gap = gap - (base - (TAPS // 2 - 1) + shift)
     out = jnp.zeros((rows, span), F32)
     for t in range(TAPS):
         out = jnp.where(gap == t, tab[f * TAPS + t], out)
@@ -75,7 +155,12 @@
     flat, flat2,
 ):
     chunks = (nv * CHIP + 2 * SEARCH + 127) // 128
-    mu, mv = nu + 2, nv + 2
+
+    def fact(kind, u, v):
+        side_u, side_v = u // nu, v // nv
+        spot = (kind * nu + u - side_u * nu) * nv + v - side_v * nv
+        return par[3 * (side_u + 1) + side_v + 1, spot]
+
     for u in range(-1, nu + 1):
         rows = CHIP if 0 <= u < nu else SEARCH
         first = u * CHIP + (CHIP - SEARCH if u < 0 else 0)
@@ -83,12 +168,11 @@
         high = min(-(-(first + LINES + rows + 12) // 16) * 16, nu * CHIP + 2 * LINES)
         totals = [None] * chunks
         for v in range(-1, nv + 1):
-            at = (u + 1) * mv + v + 1
             begin = max(v * CHIP, -SEARCH)
             end = min(v * CHIP + CHIP, nv * CHIP + SEARCH)
             left = (begin + COLS - 12) // 128 * 128
             right = left + 256
-            a = band(rows, high - low, first + LINES - low, tab, par, at, 2 * mu * mv + at)
+            a = band(rows, high - low, first + LINES - low, tab, fact(0, u, v), fact(2, u, v))
             half = jnp.concatenate(
                 [
                     jnp.dot(a, ext[c, low:high, left:right], preferred_element_type=F32)
@@ -97,7 +181,7 @@
                 axis=0,
             ).astype(BF16)
             b = band(
-                end - begin, 256, begin + COLS - left, tab, par, mu * mv + at, 3 * mu * mv + at
+                end - begin, 256, begin + COLS - left, tab, fact(1, u, v), fact(3, u, v)
             )
             spot = begin + SEARCH
             while spot < end + SEARCH:
@@ -220,13 +304,34 @@
 
 def per_device(reference_image, secondary_image, block_shifts, shift_bins, land_mask, coarse_peaks):
     nu, nv = land_mask.shape
-    par = jnp.concatenate([block_shifts, shift_bins + 1], axis=0)
-    par = with_halo(with_halo(par, "az", 1, 1), "rg", 2, 1)
-    ext = with_halo(with_halo(secondary_image, "az", 1, LINES), "rg", 2, COLS)
+    par = jnp.concatenate([block_shifts, shift_bins + 1], axis=0).reshape(1, -1)
+    par = jnp.pad(par, ((0, 0), (0, -par.shape[1] % 128)))
     smem = pl.BlockSpec(memory_space=pltpu.SMEM)
     vmem = pl.BlockSpec(memory_space=pltpu.VMEM)
     n = nu * nv
     chunks = (nv * CHIP + 2 * SEARCH + 127) // 128
+    held = (2, nu * CHIP + 2 * LINES, nv * CHIP + 2 * COLS)
+
+    def halo(*refs):
+        exchange(("az", "rg"), *refs)
+
+    par, ext = pl.pallas_call(
+        halo,
+        out_shape=(
+            jax.ShapeDtypeStruct((9, par.shape[1]), jnp.int32),
+            jax.ShapeDtypeStruct(held, BF16),
+        ),
+        in_specs=[vmem, vmem],
+        out_specs=(vmem, vmem),
+        scratch_shapes=[
+            pltpu.VMEM((9, 1, par.shape[1]), jnp.int32),
+            pltpu.VMEM(held, BF16),
+            pltpu.SemaphoreType.DMA((4, 8)),
+        ],
+        compiler_params=pltpu.CompilerParams(
+            collective_id=0, has_side_effects=True, vmem_limit_bytes=16 * 1024 * 1024
+        ),
+    )(par, secondary_image)
 
     def kernel(*refs):
         body(nu, nv, *refs)
@@ -252,7 +357,7 @@
         ],
         compiler_params=pltpu.CompilerParams(vmem_limit_bytes=48 * 1024 * 1024),
     )(
-        par.reshape(-1),
+        par,
         jnp.asarray(tap_table()),
         land_mask.reshape(-1),
         coarse_peaks.reshape(-1),

time: 46.3 us -> 27.7 us (0.60)
  the two profiles are of different devices: /device:TPU:14 before, /device:TPU:9 now
where the time goes in v2:
time: 27.7 us; the launch traced here: 27.4 us
  Pallas kernels  22.2 us (80%)
  local copies, waits for them, and re-layouts  3.21 us (12%)
  other arithmetic  1.37 us (5%)
  between operations  0.68 us (2%)
    pallas_call x1, Pallas kernels, per_device(): pl.pallas_call(kernel, out_shape=(jax.ShapeDtypeStruct((nu, nv, CHIP * CH...  12.8 us
    pallas_call x1, Pallas kernels, per_device(): pl.pallas_call(halo, out_shape=(jax.ShapeDtypeStruct((9, par.shape[1]), j...  9.33 us
    unnamed x8, local copies, waits for them, and re-layouts  1.56 us
    reshape x1, local copies, waits for them, and re-layouts, per_device(): land_mask.reshape(-1)  0.79 us
    reshape x1, local copies, waits for them, and re-layouts, per_device(): coarse_peaks.reshape(-1)  0.76 us
    concatenate x1, other arithmetic, per_device(): par = jnp.concatenate([block_shifts, shift_bins + 1], axis=0).reshape(1, -1)  0.69 us
    add x1, other arithmetic, per_device(): par = jnp.concatenate([block_shifts, shift_bins + 1], axis=0).reshape(1, -1)  0.68 us

profile of v2, /device:TPU:9, one launch (start us, length us, event | category | flops | bytes accessed | tf_op | source)
XLA Modules:
  0.0 27.4 jit_solution(13577649049197066884)
XLA Ops:
  0.6 0.0 copy-start
  0.6 0.8 %reshape.14.refs_2_ = s32[8]{0:T(128)S(1)} reshape(s32[2,4]{1,0:T(2,128)} %param.12) | data formatting | bytes 64 | tf_op jit(solution)/shard_map/reshape | solution.py:362
  1.4 0.8 %reshape.15.refs_3_ = s32[16]{0:T(128)S(1)} reshape(s32[2,2,4]{2,1,0:T(2,128)} %param.13) | data formatting | bytes 128 | tf_op jit(solution)/shard_map/reshape | solution.py:363
  2.2 0.7 %broadcast_add_fusion = s32[2,2,4]{2,1,0:T(2,128)S(1)} fusion(s32[2,2,4]{2,1,0:T(2,128)} %param.11), kind=kLoop, calls=%fused_computation.1 | loop fusion | flops 16 | bytes 128 | tf_op jit(solution)/shard_map/add | solution.py:307
  2.9 0.7 %pad_add_fusion = s32[4,2,4]{2,1,0:T(2,128)S(1)} fusion(s32[2,2,4]{2,1,0:T(2,128)S(1)} %broadcast_add_fusion, s32[2,2,4]{2,1,0:T(2,128)} %param.10), kind=kLoop, calls=%fused_computation | loop fusion | flops 32 | bytes 256 | tf_op jit(solution)/shard_map/concatenate | solution.py:307
  3.6 0.1 reshape.13
  3.7 0.0 copy-start.1
  3.7 0.9 %copy-done.1 = bf16[2,128,256]{2,1,0:T(8,128)(2,1)S(1)} copy-done((bf16[2,128,256]{2,1,0:T(8,128)(2,1)S(1)}, bf16[2,128,256]{2,1,0:T(8,128)(2,1)}, u32[]{:S(2)}) %copy-start.1) | copy-done | bytes 131096
  4.6 0.0 copy-start.2
  4.6 9.3 %shard_map.95 = (s32[9,128]{1,0:T(8,128)S(1)}, bf16[2,224,512]{2,1,0:T(8,128)(2,1)S(1)}) custom-call(s32[1,128]{1,0:T(1,128)S(1)} %pad.4.refs_0_, bf16[2,128,256]{2,1,0:T(8,128)(2,1)S(1)} %copy-done.1), custom_call_target="tpu_custom_call" | custom-call | tf_op jit(solution)/shard_map/pallas_call | solution.py:318
  13.9 0.0 copy-start.3
  13.9 0.0 copy-done
  13.9 0.0 copy-done.2
  13.9 0.7 %copy-done.3 = f32[136]{0:T(256)S(1)} copy-done((f32[136]{0:T(256)S(1)}, f32[136]{0:T(256)}, u32[]{:S(2)}) %copy-start.3) | copy-done | bytes 568
  14.6 12.8 %shard_map.96 = (f32[2,4,4096]{2,1,0:T(4,128)}, f32[2,4,1024]{2,1,0:T(4,128)}) custom-call(s32[9,128]{1,0:T(8,128)S(1)} %get-tuple-element.4.refs_0_, f32[136]{0:T(256)S(1)} %copy-done.3, s32[8]{0:T(128)S(1)} %reshape.14.refs_2_, s32[16]{0:T(128)S(1)} %reshape.15.refs_3_, bf16[2,224,512]{2,1,0:T(8,128)(2,1)S(1)} %get-tuple-element.5.refs_4_, ...), custom_call_target="tpu_custom_call" | custom-call | tf_op jit(solution)/shard_map/pallas_call | solution.py:339
  (1 shorter events, 0.0 us)
Async XLA Ops:
  0.6 13.3 %copy-start = (bf16[2,128,256]{2,1,0:T(8,128)(2,1)S(1)}, bf16[2,128,256]{2,1,0:T(8,128)(2,1)}, u32[]{:S(2)}) copy-start(bf16[2,128,256]{2,1,0:T(8,128)(2,1)} %refs_5_.1) | copy-start | bytes 393220
  3.7 0.9 %copy-start.1 = (bf16[2,128,256]{2,1,0:T(8,128)(2,1)S(1)}, bf16[2,128,256]{2,1,0:T(8,128)(2,1)}, u32[]{:S(2)}) copy-start(bf16[2,128,256]{2,1,0:T(8,128)(2,1)} %refs_1_.2) | copy-start | bytes 393220
  4.6 9.4 %copy-start.2 = (f32[32,128]{1,0:T(8,128)S(1)}, f32[32,128]{1,0:T(8,128)}, u32[]{:S(2)}) copy-start(f32[32,128]{1,0:T(8,128)} %constant.9.clone.refs_6_) | copy-start | bytes 49156
  13.9 0.7 %copy-start.3 = (f32[136]{0:T(256)S(1)}, f32[136]{0:T(256)}, u32[]{:S(2)}) copy-start(f32[136]{0:T(256)} %constant.8.clone.refs_1_) | copy-start | bytes 1636

commit v3 on v2

--- a/solution.py
+++ b/solution.py
@@ -39,7 +39,7 @@
 SIDES = [(i, j) for i in (-1, 0, 1) for j in (-1, 0, 1) if (i, j) != (0, 0)]
 
 
-def exchange(axes, par, img, out_par, out, got_par, got, sems):
+def exchange(axes, shifts, bins, img, out_par, out, par, got_par, got, sems):
     lines, cols = img.shape[1:]
     here = [lax.axis_index(a) for a in axes]
     count = [lax.axis_size(a) for a in axes]
@@ -48,6 +48,12 @@
         row, col = here[0] + i, here[1] + j
         return (row >= 0) & (row < count[0]) & (col >= 0) & (col < count[1])
 
+    rows = [shifts[k, u : u + 1, :] for k in range(2) for u in range(shifts.shape[1])]
+    rows += [bins[k, u : u + 1, :] + 1 for k in range(2) for u in range(shifts.shape[1])]
+    rest = par.shape[1] - len(rows) * shifts.shape[2]
+    if rest:
+        rows.append(jnp.zeros((1, rest), jnp.int32))
+    par[...] = jnp.concatenate(rows, axis=1)
     got[...] = jnp.zeros_like(got)
     got_par[...] = jnp.zeros_like(got_par)
     barrier = pltpu.get_barrier_semaphore()
@@ -271,14 +277,14 @@
         normed = cross / jnp.sqrt(
             energy * (squares - total * total * (1.0 / (CHIP * CHIP))) + EPSILON
         )
-        land = (mask[n] == 1) & low_lanes[:CHIP]
+        land = (mask[n // nv, n % nv] == 1) & low_lanes[:CHIP]
         surface = jnp.where(land, normed, 0.0)
         tmp[...] = surface
         pairs = tmp[pl.ds(0, 32, stride=2), :] + pltpu.roll(tmp[pl.ds(1, 32, stride=2), :], 64, 1)
         flat[n] = pairs
         lead = SEARCH - (PATCH // 2 - 1)
-        lobe_a = pltpu.roll(lobes[...], peaks[n] + lead, 1)
-        lobe_d = pltpu.roll(lobes[...], peaks[nu * nv + n] + lead, 1)
+        lobe_a = pltpu.roll(lobes[...], peaks[0, n // nv, n % nv] + lead, 1)
+        lobe_d = pltpu.roll(lobes[...], peaks[1, n // nv, n % nv] + lead, 1)
         near = jnp.dot(
             lobe_a,
             jnp.concatenate([surface, jnp.zeros((CHIP, 128), F32)], axis=0),
@@ -304,8 +310,7 @@
 
 def per_device(reference_image, secondary_image, block_shifts, shift_bins, land_mask, coarse_peaks):
     nu, nv = land_mask.shape
-    par = jnp.concatenate([block_shifts, shift_bins + 1], axis=0).reshape(1, -1)
-    par = jnp.pad(par, ((0, 0), (0, -par.shape[1] % 128)))
+    facts = -(-4 * nu * nv // 128) * 128
     smem = pl.BlockSpec(memory_space=pltpu.SMEM)
     vmem = pl.BlockSpec(memory_space=pltpu.VMEM)
     n = nu * nv
@@ -318,20 +323,21 @@
     par, ext = pl.pallas_call(
         halo,
         out_shape=(
-            jax.ShapeDtypeStruct((9, par.shape[1]), jnp.int32),
+            jax.ShapeDtypeStruct((9, facts), jnp.int32),
             jax.ShapeDtypeStruct(held, BF16),
         ),
-        in_specs=[vmem, vmem],
+        in_specs=[vmem, vmem, vmem],
         out_specs=(vmem, vmem),
         scratch_shapes=[
-            pltpu.VMEM((9, 1, par.shape[1]), jnp.int32),
+            pltpu.VMEM((1, facts), jnp.int32),
+            pltpu.VMEM((9, 1, facts), jnp.int32),
             pltpu.VMEM(held, BF16),
             pltpu.SemaphoreType.DMA((4, 8)),
         ],
         compiler_params=pltpu.CompilerParams(
             collective_id=0, has_side_effects=True, vmem_limit_bytes=16 * 1024 * 1024
         ),
-    )(par, secondary_image)
+    )(block_shifts, shift_bins, secondary_image)
 
     def kernel(*refs):
         body(nu, nv, *refs)
@@ -359,8 +365,8 @@
     )(
         par,
         jnp.asarray(tap_table()),
-        land_mask.reshape(-1),
-        coarse_peaks.reshape(-1),
+        land_mask,
+        coarse_peaks,
         ext,
         reference_image,
         jnp.asarray(lobe_table()),

time: 27.7 us -> 26.9 us (0.971)
  other arithmetic: 1.37 us -> 0 us
  local copies, waits for them, and re-layouts: 3.21 us -> 3.65 us
    unnamed x8 -> x16, local copies, waits for them, and re-layouts: 1.56 us -> 3.65 us
    reshape x3 -> x0, local copies, waits for them, and re-layouts: 1.64 us -> none  [the longest x1 0.79 us: per_device(): land_mask.reshape(-1)]
    concatenate x1 -> x0, other arithmetic: 0.69 us -> none  [per_device(): par = jnp.concatenate([block_shifts, shift_bins + 1], axis=0).reshape(1, -1)]
    add x1 -> x0, other arithmetic: 0.68 us -> none  [per_device(): par = jnp.concatenate([block_shifts, shift_bins + 1], axis=0).reshape(1, -1)]
where the time goes in v3:
time: 26.9 us; the launch traced here: 26.6 us
  Pallas kernels  22.3 us (83%)
  local copies, waits for them, and re-layouts  3.65 us (14%)
  between operations  0.68 us (3%)
    pallas_call x1, Pallas kernels, per_device(): pl.pallas_call(kernel, out_shape=(jax.ShapeDtypeStruct((nu, nv, CHIP * CH...  12.9 us
    pallas_call x1, Pallas kernels, per_device(): pl.pallas_call(halo, out_shape=(jax.ShapeDtypeStruct((9, facts), jnp.int3...  9.36 us
    unnamed x16, local copies, waits for them, and re-layouts  3.65 us

profile of v3, /device:TPU:9, one launch (start us, length us, event | category | flops | bytes accessed | tf_op | source)
XLA Modules:
  0.0 26.6 jit_solution(13385384402105852729)
XLA Ops:
  0.6 0.0 copy-start.1
  0.6 0.9 %copy-done.1 = bf16[2,128,256]{2,1,0:T(8,128)(2,1)S(1)} copy-done((bf16[2,128,256]{2,1,0:T(8,128)(2,1)S(1)}, bf16[2,128,256]{2,1,0:T(8,128)(2,1)}, u32[]{:S(2)}) %copy-start.1) | copy-done | bytes 131096
  1.5 0.0 copy-start.3
  1.5 0.7 %copy-done.3 = s32[2,2,4]{2,1,0:T(2,128)S(1)} copy-done((s32[2,2,4]{2,1,0:T(2,128)S(1)}, s32[2,2,4]{2,1,0:T(2,128)}, u32[]{:S(2)}) %copy-start.3) | copy-done | bytes 88
  2.2 0.0 copy-start.4
  2.2 0.7 %copy-done.4 = s32[2,2,4]{2,1,0:T(2,128)S(1)} copy-done((s32[2,2,4]{2,1,0:T(2,128)S(1)}, s32[2,2,4]{2,1,0:T(2,128)}, u32[]{:S(2)}) %copy-start.4) | copy-done | bytes 88
  2.9 0.0 copy-start
  2.9 0.0 copy-start.7
  2.9 9.4 %shard_map.95 = (s32[9,128]{1,0:T(8,128)S(1)}, bf16[2,224,512]{2,1,0:T(8,128)(2,1)S(1)}) custom-call(s32[2,2,4]{2,1,0:T(2,128)S(1)} %copy-done.3, s32[2,2,4]{2,1,0:T(2,128)S(1)} %copy-done.4, bf16[2,128,256]{2,1,0:T(8,128)(2,1)S(1)} %copy-done.1), custom_call_target="tpu_custom_call" | custom-call | tf_op jit(solution)/shard_map/pallas_call | solution.py:323
  12.3 0.0 copy-start.5
  12.3 0.0 copy-start.6
  12.3 0.0 copy-done
  12.3 0.0 copy-done.7
  12.3 0.6 %copy-done.5 = s32[2,2,4]{2,1,0:T(2,128)S(1)} copy-done((s32[2,2,4]{2,1,0:T(2,128)S(1)}, s32[2,2,4]{2,1,0:T(2,128)}, u32[]{:S(2)}) %copy-start.5) | copy-done | bytes 88
  13.0 0.0 copy-done.6
  13.0 0.0 copy-start.2
  13.0 0.7 %copy-done.2 = f32[32,128]{1,0:T(8,128)S(1)} copy-done((f32[32,128]{1,0:T(8,128)S(1)}, f32[32,128]{1,0:T(8,128)}, u32[]{:S(2)}) %copy-start.2) | copy-done | bytes 16408
  13.7 12.9 %shard_map.96 = (f32[2,4,4096]{2,1,0:T(4,128)}, f32[2,4,1024]{2,1,0:T(4,128)}) custom-call(s32[9,128]{1,0:T(8,128)S(1)} %get-tuple-element.4.refs_0_, f32[136]{0:T(256)S(1)} %copy-done.7, s32[2,4]{1,0:T(2,128)S(1)} %copy-done.6, s32[2,2,4]{2,1,0:T(2,128)S(1)} %copy-done.5, bf16[2,224,512]{2,1,0:T(8,128)(2,1)S(1)} %get-tuple-element.5.refs_4_, ...), custom_call_target="tpu_custom_call" | custom-call | tf_op jit(solution)/shard_map/pallas_call | solution.py:345
Async XLA Ops:
  0.6 0.9 %copy-start.1 = (bf16[2,128,256]{2,1,0:T(8,128)(2,1)S(1)}, bf16[2,128,256]{2,1,0:T(8,128)(2,1)}, u32[]{:S(2)}) copy-start(bf16[2,128,256]{2,1,0:T(8,128)(2,1)} %refs_2_.2) | copy-start | bytes 393220
  1.5 0.7 %copy-start.3 = (s32[2,2,4]{2,1,0:T(2,128)S(1)}, s32[2,2,4]{2,1,0:T(2,128)}, u32[]{:S(2)}) copy-start(s32[2,2,4]{2,1,0:T(2,128)} %refs_0_.1) | copy-start | bytes 196
  2.2 0.7 %copy-start.4 = (s32[2,2,4]{2,1,0:T(2,128)S(1)}, s32[2,2,4]{2,1,0:T(2,128)}, u32[]{:S(2)}) copy-start(s32[2,2,4]{2,1,0:T(2,128)} %refs_1_.2) | copy-start | bytes 196
  2.9 9.4 %copy-start = (bf16[2,128,256]{2,1,0:T(8,128)(2,1)S(1)}, bf16[2,128,256]{2,1,0:T(8,128)(2,1)}, u32[]{:S(2)}) copy-start(bf16[2,128,256]{2,1,0:T(8,128)(2,1)} %refs_5_.1) | copy-start | bytes 393220
  2.9 9.4 %copy-start.7 = (f32[136]{0:T(256)S(1)}, f32[136]{0:T(256)}, u32[]{:S(2)}) copy-start(f32[136]{0:T(256)} %constant.4.clone.refs_1_) | copy-start | bytes 1636
  12.3 0.7 %copy-start.5 = (s32[2,2,4]{2,1,0:T(2,128)S(1)}, s32[2,2,4]{2,1,0:T(2,128)}, u32[]{:S(2)}) copy-start(s32[2,2,4]{2,1,0:T(2,128)} %refs_3_.1) | copy-start | bytes 196
  12.3 0.7 %copy-start.6 = (s32[2,4]{1,0:T(2,128)S(1)}, s32[2,4]{1,0:T(2,128)}, u32[]{:S(2)}) copy-start(s32[2,4]{1,0:T(2,128)} %refs_2_.3) | copy-start | bytes 100
  13.0 0.7 %copy-start.2 = (f32[32,128]{1,0:T(8,128)S(1)}, f32[32,128]{1,0:T(8,128)}, u32[]{:S(2)}) copy-start(f32[32,128]{1,0:T(8,128)} %constant.5.clone.refs_6_) | copy-start | bytes 49156

commit v4 on v3

--- a/solution.py
+++ b/solution.py
@@ -39,7 +39,9 @@
 SIDES = [(i, j) for i in (-1, 0, 1) for j in (-1, 0, 1) if (i, j) != (0, 0)]
 
 
-def exchange(axes, shifts, bins, img, out_par, out, par, got_par, got, sems):
+def exchange(
+    axes, far_shifts, far_bins, far_img, out_par, out, shifts, bins, img, near_sems, par, got_par, got, sems
+):
     lines, cols = img.shape[1:]
     here = [lax.axis_index(a) for a in axes]
     count = [lax.axis_size(a) for a in axes]
@@ -48,12 +50,14 @@
         row, col = here[0] + i, here[1] + j
         return (row >= 0) & (row < count[0]) & (col >= 0) & (col < count[1])
 
-    rows = [shifts[k, u : u + 1, :] for k in range(2) for u in range(shifts.shape[1])]
-    rows += [bins[k, u : u + 1, :] + 1 for k in range(2) for u in range(shifts.shape[1])]
-    rest = par.shape[1] - len(rows) * shifts.shape[2]
-    if rest:
-        rows.append(jnp.zeros((1, rest), jnp.int32))
-    par[...] = jnp.concatenate(rows, axis=1)
+    loads = [
+        pltpu.make_async_copy(far, near, near_sems.at[k])
+        for k, (far, near) in enumerate(
+            ((far_img, img), (far_shifts, shifts), (far_bins, bins))
+        )
+    ]
+    for load in loads:
+        load.start()
     got[...] = jnp.zeros_like(got)
     got_par[...] = jnp.zeros_like(got_par)
     barrier = pltpu.get_barrier_semaphore()
@@ -71,6 +75,14 @@
     tall, wide = (
         1 + jnp.where(h > 0, 1, 0) + jnp.where(h < n - 1, 1, 0) for h, n in zip(here, count)
     )
+    for load in loads:
+        load.wait()
+    rows = [shifts[k, u : u + 1, :] for k in range(2) for u in range(shifts.shape[1])]
+    rows += [bins[k, u : u + 1, :] + 1 for k in range(2) for u in range(shifts.shape[1])]
+    rest = par.shape[1] - len(rows) * shifts.shape[2]
+    if rest:
+        rows.append(jnp.zeros((1, rest), jnp.int32))
+    par[...] = jnp.concatenate(rows, axis=1)
     pl.semaphore_wait(barrier, tall * wide - 1)
 
     def spans(step, size, width):
@@ -326,16 +338,20 @@
             jax.ShapeDtypeStruct((9, facts), jnp.int32),
             jax.ShapeDtypeStruct(held, BF16),
         ),
-        in_specs=[vmem, vmem, vmem],
+        in_specs=[pl.BlockSpec(memory_space=pltpu.HBM)] * 3,
         out_specs=(vmem, vmem),
         scratch_shapes=[
+            pltpu.VMEM(block_shifts.shape, jnp.int32),
+            pltpu.VMEM(shift_bins.shape, jnp.int32),
+            pltpu.VMEM(secondary_image.shape, BF16),
+            pltpu.SemaphoreType.DMA((3,)),
             pltpu.VMEM((1, facts), jnp.int32),
             pltpu.VMEM((9, 1, facts), jnp.int32),
             pltpu.VMEM(held, BF16),
             pltpu.SemaphoreType.DMA((4, 8)),
         ],
         compiler_params=pltpu.CompilerParams(
-            collective_id=0, has_side_effects=True, vmem_limit_bytes=16 * 1024 * 1024
+            collective_id=0, has_side_effects=True, vmem_limit_bytes=63 * 1024 * 1024
         ),
     )(block_shifts, shift_bins, secondary_image)
 
@@ -361,7 +377,7 @@
             pltpu.VMEM((n, CHIP // 2, 128), F32),
             pltpu.VMEM((n, 8, 128), F32),
         ],
-        compiler_params=pltpu.CompilerParams(vmem_limit_bytes=48 * 1024 * 1024),
+        compiler_params=pltpu.CompilerParams(vmem_limit_bytes=63 * 1024 * 1024),
     )(
         par,
         jnp.asarray(tap_table()),

time: 26.9 us -> 24.2 us (0.90)
  local copies, waits for them, and re-layouts: 3.65 us -> 0 us
  Pallas kernels: 22.3 us -> 23.4 us
    unnamed x16 -> x0, local copies, waits for them, and re-layouts: 3.65 us -> none
    pallas_call x1, Pallas kernels: 9.36 us -> 10.1 us  [per_device(): pl.pallas_call(halo, out_shape=(jax.ShapeDtypeStruct((9, facts), jnp.int3...]
    pallas_call x1, Pallas kernels: 12.9 us -> 13.3 us  [per_device(): pl.pallas_call(kernel, out_shape=(jax.ShapeDtypeStruct((nu, nv, CHIP * CH...]
where the time goes in v4:
time: 24.2 us; the launch traced here: 24 us
  Pallas kernels  23.4 us (97%)
  between operations  0.64 us (3%)
    pallas_call x1, Pallas kernels, per_device(): pl.pallas_call(kernel, out_shape=(jax.ShapeDtypeStruct((nu, nv, CHIP * CH...  13.3 us
    pallas_call x1, Pallas kernels, per_device(): pl.pallas_call(halo, out_shape=(jax.ShapeDtypeStruct((9, facts), jnp.int3...  10.1 us

profile of v4, /device:TPU:9, one launch (start us, length us, event | category | flops | bytes accessed | tf_op | source)
XLA Modules:
  0.0 24.0 jit_solution(13705957480192419136)
XLA Ops:
  0.6 10.1 %shard_map.95 = (s32[9,128]{1,0:T(8,128)}, bf16[2,224,512]{2,1,0:T(8,128)(2,1)}) custom-call(s32[2,2,4]{2,1,0:T(2,128)} %refs_0_.1, s32[2,2,4]{2,1,0:T(2,128)} %refs_1_.2, bf16[2,128,256]{2,1,0:T(8,128)(2,1)} %refs_2_.2), custom_call_target="tpu_custom_call" | custom-call | tf_op jit(solution)/shard_map/pallas_call | solution.py:335
  10.8 13.3 %shard_map.96 = (f32[2,4,4096]{2,1,0:T(4,128)}, f32[2,4,1024]{2,1,0:T(4,128)}) custom-call(s32[9,128]{1,0:T(8,128)} %get-tuple-element.4.refs_0_, f32[136]{0:T(256)} %constant.4.clone.refs_1_, s32[2,4]{1,0:T(2,128)} %refs_2_.3, s32[2,2,4]{2,1,0:T(2,128)} %refs_3_.1, bf16[2,224,512]{2,1,0:T(8,128)(2,1)} %get-tuple-element.5.refs_4_, ...), custom_call_target="tpu_custom_call" | custom-call | tf_op jit(solution)/shard_map/pallas_call | solution.py:361

commit v5 on v4

--- a/solution.py
+++ b/solution.py
@@ -256,7 +256,7 @@
     gap_c = lax.broadcasted_iota(jnp.int32, (128, 128), 0) - lane
     ones_c = jnp.where((gap_c >= 0) & (gap_c < CHIP), 1.0, 0.0).astype(BF16)
 
-    def one_chip(n, carry):
+    def one_chip(n, wts, toep, tmp, tmp2):
         w = win[n]
         for s in range(GROUP):
             shifted = pltpu.roll(w, 128 - s, 1) if s else w
@@ -309,9 +309,14 @@
         for r in range(1, 4):
             quads = quads + pltpu.roll(tmp2[pl.ds(r, 8, stride=4), :], 32 * r, 1)
         flat2[n] = quads
+
+    def one_turn(turn, carry):
+        for b in range(turns):
+            one_chip(turn * turns + b, wts.at[b], toep.at[b], tmp.at[b], tmp2.at[b])
         return carry
 
-    lax.fori_loop(0, nu * nv, one_chip, 0)
+    turns = wts.shape[0]
+    lax.fori_loop(0, nu * nv // turns, one_turn, 0)
     for u in range(nu):
         for v in range(nv):
             for m in range(CHIP // 2):
@@ -326,6 +331,7 @@
     smem = pl.BlockSpec(memory_space=pltpu.SMEM)
     vmem = pl.BlockSpec(memory_space=pltpu.VMEM)
     n = nu * nv
+    turns = 2 if n % 2 == 0 else 1
     chunks = (nv * CHIP + 2 * SEARCH + 127) // 128
     held = (2, nu * CHIP + 2 * LINES, nv * CHIP + 2 * COLS)
 
@@ -370,10 +376,10 @@
             pltpu.VMEM((nu * CHIP + 2 * SEARCH, chunks * 128), F32),
             pltpu.VMEM((n, 2 * CHIP, 128), F32),
             pltpu.VMEM((n, CHIP, 128), F32),
-            pltpu.VMEM((GROUP * 128, 128), BF16),
-            pltpu.VMEM((CHIP * CHIP // GROUP, GROUP * 128), BF16),
-            pltpu.VMEM((CHIP, 128), F32),
-            pltpu.VMEM((2 * OVERS, 128), F32),
+            pltpu.VMEM((turns, GROUP * 128, 128), BF16),
+            pltpu.VMEM((turns, CHIP * CHIP // GROUP, GROUP * 128), BF16),
+            pltpu.VMEM((turns, CHIP, 128), F32),
+            pltpu.VMEM((turns, 2 * OVERS, 128), F32),
             pltpu.VMEM((n, CHIP // 2, 128), F32),
             pltpu.VMEM((n, 8, 128), F32),
         ],

time: 24.2 us -> 23.9 us (0.988)
  Pallas kernels: 23.4 us -> 23.1 us
    pallas_call x1, Pallas kernels: 13.3 us -> 12.9 us  [per_device(): pl.pallas_call(kernel, out_shape=(jax.ShapeDtypeStruct((nu, nv, CHIP * CH...]
where the time goes in v5:
time: 23.9 us; the launch traced here: 23.7 us
  Pallas kernels  23.1 us (97%)
  between operations  0.64 us (3%)
    pallas_call x1, Pallas kernels, per_device(): pl.pallas_call(kernel, out_shape=(jax.ShapeDtypeStruct((nu, nv, CHIP * CH...  12.9 us
    pallas_call x1, Pallas kernels, per_device(): pl.pallas_call(halo, out_shape=(jax.ShapeDtypeStruct((9, facts), jnp.int3...  10.1 us

profile of v5, /device:TPU:9, one launch (start us, length us, event | category | flops | bytes accessed | tf_op | source)
XLA Modules:
  0.0 23.7 jit_solution(4238639175354336337)
XLA Ops:
  0.6 10.1 %shard_map.95 = (s32[9,128]{1,0:T(8,128)}, bf16[2,224,512]{2,1,0:T(8,128)(2,1)}) custom-call(s32[2,2,4]{2,1,0:T(2,128)} %refs_0_.1, s32[2,2,4]{2,1,0:T(2,128)} %refs_1_.2, bf16[2,128,256]{2,1,0:T(8,128)(2,1)} %refs_2_.2), custom_call_target="tpu_custom_call" | custom-call | tf_op jit(solution)/shard_map/pallas_call | solution.py:341
  10.8 12.9 %shard_map.96 = (f32[2,4,4096]{2,1,0:T(4,128)}, f32[2,4,1024]{2,1,0:T(4,128)}) custom-call(s32[9,128]{1,0:T(8,128)} %get-tuple-element.4.refs_0_, f32[136]{0:T(256)} %constant.4.clone.refs_1_, s32[2,4]{1,0:T(2,128)} %refs_2_.3, s32[2,2,4]{2,1,0:T(2,128)} %refs_3_.1, bf16[2,224,512]{2,1,0:T(8,128)(2,1)} %get-tuple-element.5.refs_4_, ...), custom_call_target="tpu_custom_call" | custom-call | tf_op jit(solution)/shard_map/pallas_call | solution.py:367

commit v6 on v5

--- a/solution.py
+++ b/solution.py
@@ -331,7 +331,7 @@
     smem = pl.BlockSpec(memory_space=pltpu.SMEM)
     vmem = pl.BlockSpec(memory_space=pltpu.VMEM)
     n = nu * nv
-    turns = 2 if n % 2 == 0 else 1
+    turns = next(t for t in (4, 2, 1) if n % t == 0)
     chunks = (nv * CHIP + 2 * SEARCH + 127) // 128
     held = (2, nu * CHIP + 2 * LINES, nv * CHIP + 2 * COLS)
 

time: 23.9 us -> 22.6 us (0.946)
  Pallas kernels: 23.1 us -> 21.8 us
    pallas_call x1, Pallas kernels: 12.9 us -> 11.7 us  [per_device(): pl.pallas_call(kernel, out_shape=(jax.ShapeDtypeStruct((nu, nv, CHIP * CH...]
where the time goes in v6:
time: 22.6 us; the launch traced here: 22.5 us
  Pallas kernels  21.8 us (96%)
  between operations  0.64 us (3%)
    pallas_call x1, Pallas kernels, per_device(): pl.pallas_call(kernel, out_shape=(jax.ShapeDtypeStruct((nu, nv, CHIP * CH...  11.7 us
    pallas_call x1, Pallas kernels, per_device(): pl.pallas_call(halo, out_shape=(jax.ShapeDtypeStruct((9, facts), jnp.int3...  10.1 us

profile of v6, /device:TPU:9, one launch (start us, length us, event | category | flops | bytes accessed | tf_op | source)
XLA Modules:
  0.0 22.5 jit_solution(1181810115871885371)
XLA Ops:
  0.6 10.1 %shard_map.95 = (s32[9,128]{1,0:T(8,128)}, bf16[2,224,512]{2,1,0:T(8,128)(2,1)}) custom-call(s32[2,2,4]{2,1,0:T(2,128)} %refs_0_.1, s32[2,2,4]{2,1,0:T(2,128)} %refs_1_.2, bf16[2,128,256]{2,1,0:T(8,128)(2,1)} %refs_2_.2), custom_call_target="tpu_custom_call" | custom-call | tf_op jit(solution)/shard_map/pallas_call | solution.py:341
  10.8 11.7 %shard_map.96 = (f32[2,4,4096]{2,1,0:T(4,128)}, f32[2,4,1024]{2,1,0:T(4,128)}) custom-call(s32[9,128]{1,0:T(8,128)} %get-tuple-element.4.refs_0_, f32[136]{0:T(256)} %constant.4.clone.refs_1_, s32[2,4]{1,0:T(2,128)} %refs_2_.3, s32[2,2,4]{2,1,0:T(2,128)} %refs_3_.1, bf16[2,224,512]{2,1,0:T(8,128)(2,1)} %get-tuple-element.5.refs_4_, ...), custom_call_target="tpu_custom_call" | custom-call | tf_op jit(solution)/shard_map/pallas_call | solution.py:367
